TPU v7x, 512 devices: a whole 4x8x8 slice. The times are simulated.
512 devices in a mesh: row: 16 (over x_hi, z), col: 16 (over y, core), rep: 2 (over x_lo).
Axes of the slice: x: 4 (x_hi: 2, x_lo: 2; x = x_hi * 2 + x_lo), y: 8, z: 8, core: 2. Of those that a mesh axis runs over, the one named last changes fastest.
Arguments:
- grad_parts: bfloat16 [2, 4608, 4608], P('rep', 'row', 'col'), may hold values from -6 to 6
- basis_left: bfloat16 [4608, 4608], P(('col', 'rep'), 'row'), may hold values from -0.09375 to 0.09375
- basis_right: bfloat16 [4608, 4608], P(('row', 'rep'), 'col'), may hold values from -0.09375 to 0.09375
- first_moment: float32 [4608, 4608], P(('row', 'rep'), 'col'), may hold values from -6 to 6
- second_moment: float32 [4608, 4608], P(('row', 'rep'), 'col'), may hold values from 0.5 to 4
Outputs:
- update: float32 [4608, 4608], P(('row', 'rep'), 'col')
- new_first: float32 [4608, 4608], P(('row', 'rep'), 'col')
- new_second: float32 [4608, 4608], P(('row', 'rep'), 'col')
All inputs are finite; a program needn't handle non-finite values.
Results may differ from a plain program's by a relative error of at most 0.0041.
Values may be sent and summed in bfloat16 or wider, within the bound.
No kernel may reach another device: no remote copies, remote signals or barrier semaphores. Data moves between devices by JAX's collectives and lax.ppermute only.
A program may use at most 64 MiB of HBM per device.

v0:
```python
import jax
import jax.numpy as jnp
from jax import lax
from jax.sharding import PartitionSpec as P

BETA_ONE = 0.9
BETA_TWO = 0.95
EPSILON = 1e-08


def from_root(block, axis, holder):
    block = jnp.where(lax.axis_index(axis) == holder, block, jnp.zeros_like(block))
    return lax.psum(block, axis)


def on_device(grad_parts, basis_left, basis_right, first_moment, second_moment):
    grad_tile = grad_parts[0].astype(jnp.float32)
    grad_half = lax.psum_scatter(
        grad_tile.astype(jnp.bfloat16), "rep", scatter_dimension=0, tiled=True
    )
    grad_panel = lax.all_gather(grad_half, "row", axis=0, tiled=True)
    matched = grad_panel
    first_part = jnp.einsum(
        "kr,kc->rc",
        lax.all_gather(basis_left, "col", axis=0, tiled=True),
        matched,
        preferred_element_type=jnp.float32,
    )
    rotated = lax.psum_scatter(first_part, "rep", scatter_dimension=1, tiled=True).astype(
        jnp.bfloat16
    )
    rotated_panel = lax.all_gather(rotated, "col", axis=1, tiled=True)
    matched = rotated_panel
    second_part = jnp.dot(
        matched,
        lax.all_gather(basis_right, "row", axis=0, tiled=True),
        preferred_element_type=jnp.float32,
    )
    projected = lax.psum_scatter(second_part, "rep", scatter_dimension=0, tiled=True)
    new_first = BETA_ONE * first_moment + (1.0 - BETA_ONE) * projected
    new_second = BETA_TWO * second_moment + (1.0 - BETA_TWO) * projected * projected
    normed = (new_first / (jnp.sqrt(new_second) + EPSILON)).astype(jnp.bfloat16)
    normed_panel = lax.all_gather(normed, "row", axis=0, tiled=True)
    left_parts = lax.all_to_all(basis_left, "rep", split_axis=1, concat_axis=0, tiled=True)
    left_rows = lax.all_gather(left_parts, "row", axis=1, tiled=True)
    left_rows = from_root(left_rows, "col", lax.axis_index("row"))
    third_part = jnp.dot(left_rows, normed_panel, preferred_element_type=jnp.float32)
    back_left = lax.psum_scatter(third_part, "rep", scatter_dimension=1, tiled=True).astype(
        jnp.bfloat16
    )
    back_panel = lax.all_gather(back_left, "col", axis=1, tiled=True)
    right_parts = lax.all_to_all(basis_right, "rep", split_axis=1, concat_axis=0, tiled=True)
    right_rows = lax.all_gather(right_parts, "col", axis=1, tiled=True)
    right_rows = from_root(right_rows, "row", lax.axis_index("col"))
    fourth_part = jnp.einsum(
        "rk,ck->rc", back_panel, right_rows, preferred_element_type=jnp.float32
    )
    update = lax.psum_scatter(fourth_part, "rep", scatter_dimension=0, tiled=True)
    return (update, new_first, new_second)


def solution(mesh):
    in_specs = (
        P("rep", "row", "col"),
        P(("col", "rep"), "row"),
        P(("row", "rep"), "col"),
        P(("row", "rep"), "col"),
        P(("row", "rep"), "col"),
    )
    out_specs = (P(("row", "rep"), "col"), P(("row", "rep"), "col"), P(("row", "rep"), "col"))
    return jax.shard_map(
        on_device, mesh=mesh, in_specs=in_specs, out_specs=out_specs, check_vma=False
    )
```

profile of v0, /device:TPU:1, one launch (start us, length us, event | category | flops | bytes accessed | tf_op | source)
XLA Modules:
  0.0 877.3 jit_solution(12139021195884002302)
XLA Ops:
  8.0 0.0 reduce-scatter.10.cloned.1.call-start
  8.0 0.7 reduce-scatter.10.cloned.1.call-update
  8.7 0.0 all-gather.11.cloned.1.call-start
  8.8 0.5 all-gather.11.cloned.1.call-update
  9.3 0.0 all-gather.13.cloned.1.call-start
  9.4 26.9 %reduce-scatter.10.cloned.1.call-done = bf16[144,288]{1,0:T(8,128)(2,1)} async-done(((bf16[288,288]{1,0:T(8,128)(2,1)}), bf16[144,288]{1,0:T(8,128)(2,1)}) %reduce-scatter.10.cloned.1.call-update) | async-done | bytes 82960 | tf_op jit(solution)/shard_map/reduce_scatter | solution.py:18
  36.2 0.0 all-gather.13.cloned.1.call-update
  36.3 0.0 reduce-scatter.16.cloned.1.call-start
  36.3 22.6 %all-gather.11.cloned.1.call-done = bf16[2304,288]{1,0:T(8,128)(2,1)} async-done(((bf16[144,288]{1,0:T(8,128)(2,1)}), bf16[2304,288]{1,0:T(8,128)(2,1)}) %all-gather.11.cloned.1.call-update) | async-done | bytes 1327120 | tf_op jit(solution)/shard_map/all_gather | solution.py:25
  58.9 87.9 %all-gather.13.cloned.1.call-done = bf16[2304,288]{1,0:T(8,128)(2,1)} async-done(((bf16[144,288]{1,0:T(8,128)(2,1)}), bf16[2304,288]{1,0:T(8,128)(2,1)}) %all-gather.13.cloned.1.call-update) | async-done | bytes 1327120 | tf_op jit(solution)/shard_map/all_gather | solution.py:21
  146.8 3.7 convolution_bitcast_fusion.1
  150.5 0.0 reduce-scatter.16.cloned.1.call-update
  150.5 0.0 all-gather.17.cloned.1.call-start
  150.6 0.5 all-gather.17.cloned.1.call-update
  151.1 0.0 all-gather.15.cloned.1.call-start
  151.1 21.2 %reduce-scatter.16.cloned.1.call-done = f32[144,288]{1,0:T(8,128)} async-done(((f32[288,288]{1,0:T(8,128)}), f32[144,288]{1,0:T(8,128)}) %reduce-scatter.16.cloned.1.call-update) | async-done | bytes 165904
  172.4 1.6 bitcast_convert_fusion.1
  174.0 0.0 all-gather.15.cloned.1.call-update
  174.0 0.0 all-gather.9.cloned.1.call-start
  174.1 0.1 copy.18
  174.2 5.8 all_to_all.38
  179.9 0.1 copy.19
  180.1 0.8 all_to_all.31
  180.8 0.0 all-gather.9.cloned.1.call-update
  180.9 0.0 reduce-scatter.12.cloned.1.call-start
  180.9 59.9 %all-gather.17.cloned.1.call-done = bf16[2304,288]{1,0:T(8,128)(2,1)} async-done(((bf16[144,288]{1,0:T(8,128)(2,1)}), bf16[2304,288]{1,0:T(8,128)(2,1)}) %all-gather.17.cloned.1.call-update) | async-done | bytes 1327120 | tf_op jit(solution)/shard_map/all_gather | solution.py:36
  240.8 45.2 %all-gather.15.cloned.1.call-done = bf16[288,2304]{0,1:T(8,128)(2,1)} async-done(((bf16[288,144]{0,1:T(8,128)(2,1)}), bf16[288,2304]{0,1:T(8,128)(2,1)}) %all-gather.15.cloned.1.call-update) | async-done | bytes 1327120 | tf_op jit(solution)/shard_map/all_gather | solution.py:32
  286.0 3.7 fusion.2
  289.6 0.0 reduce-scatter.12.cloned.1.call-update
  289.6 0.0 all-reduce.3.cloned.1.call-start
  289.7 87.6 %all-gather.9.cloned.1.call-done = bf16[288,2304]{0,1:T(8,128)(2,1)} async-done(((bf16[288,144]{0,1:T(8,128)(2,1)}), bf16[288,2304]{0,1:T(8,128)(2,1)}) %all-gather.9.cloned.1.call-update) | async-done | bytes 1327120 | tf_op jit(solution)/shard_map/all_gather | solution.py:45
  377.3 1.4 broadcast_select_fusion.1
  378.7 0.0 all-reduce.3.cloned.1.call-update
  378.7 0.0 all-gather.19.cloned.1.call-start
  378.8 0.0 reduce-scatter.12.cloned.1.call-done
  378.8 0.8 copy-done.2
  379.6 0.1 copy-done.3
  379.7 1.8 divide_convert_fusion
  381.5 0.0 all-gather.19.cloned.1.call-update
  381.6 0.0 all-gather.23.cloned.1.call-start
  381.6 0.1 copy.24
  381.7 5.8 all_to_all.39
  387.5 0.1 copy.25
  387.6 0.8 all_to_all.35
  388.4 0.0 all-gather.23.cloned.1.call-update
  388.4 0.0 reduce-scatter.18.cloned.1.call-start
  388.5 109.9 %all-reduce.3.cloned.1.call-done = bf16[288,2304]{0,1:T(8,128)(2,1)} async-done(((bf16[288,2304]{0,1:T(8,128)(2,1)}), bf16[288,2304]{0,1:T(8,128)(2,1)}) %all-reduce.3.cloned.1.call-update) | async-done | bytes 1327120 | tf_op jit(solution)/shard_map/psum | solution.py:13
  498.4 91.2 %all-gather.19.cloned.1.call-done = bf16[2304,288]{1,0:T(8,128)(2,1)} async-done(((bf16[144,288]{1,0:T(8,128)(2,1)}), bf16[2304,288]{1,0:T(8,128)(2,1)}) %all-gather.19.cloned.1.call-update) | async-done | bytes 1327120 | tf_op jit(solution)/shard_map/all_gather | solution.py:43
  589.6 3.7 convolution_bitcast_fusion
  593.3 0.0 reduce-scatter.18.cloned.1.call-update
  593.3 0.0 all-reduce.5.cloned.1.call-start
  593.4 40.4 %all-gather.23.cloned.1.call-done = bf16[288,2304]{0,1:T(8,128)(2,1)} async-done(((bf16[288,144]{0,1:T(8,128)(2,1)}), bf16[288,2304]{0,1:T(8,128)(2,1)}) %all-gather.23.cloned.1.call-update) | async-done | bytes 1327120 | tf_op jit(solution)/shard_map/all_gather | solution.py:53
  633.8 1.4 broadcast_select_fusion
  635.2 0.0 all-reduce.5.cloned.1.call-update
  635.2 0.0 all-gather.21.cloned.1.call-start
  635.3 0.0 reduce-scatter.18.cloned.1.call-done
  635.3 1.6 bitcast_convert_fusion
  636.9 0.0 all-gather.21.cloned.1.call-update
  636.9 0.0 reduce-scatter.14.cloned.1.call-start
  637.0 155.6 %all-reduce.5.cloned.1.call-done = bf16[288,2304]{0,1:T(8,128)(2,1)} async-done(((bf16[288,2304]{0,1:T(8,128)(2,1)}), bf16[288,2304]{0,1:T(8,128)(2,1)}) %all-reduce.5.cloned.1.call-update) | async-done | bytes 1327120 | tf_op jit(solution)/shard_map/psum | solution.py:13
  792.6 53.3 %all-gather.21.cloned.1.call-done = bf16[288,2304]{0,1:T(8,128)(2,1)} async-done(((bf16[288,144]{0,1:T(8,128)(2,1)}), bf16[288,2304]{0,1:T(8,128)(2,1)}) %all-gather.21.cloned.1.call-update) | async-done | bytes 1327120 | tf_op jit(solution)/shard_map/all_gather | solution.py:51
  845.9 3.7 fusion.3
  849.6 0.0 reduce-scatter.14.cloned.1.call-update
  849.6 20.6 %reduce-scatter.14.cloned.1.call-done = f32[144,288]{1,0:T(8,128)} async-done(((f32[288,288]{1,0:T(8,128)}), f32[144,288]{1,0:T(8,128)}) %reduce-scatter.14.cloned.1.call-update) | async-done | bytes 165904 | tf_op jit(solution)/shard_map/reduce_scatter | solution.py:58
  (6 shorter events, 0.0 us)
Async XLA Ops:
  8.0 28.2 %reduce-scatter.10.cloned.1.call-start = ((), (), s32[]{:S(2)}) async-start(), calls=%async_computation.10 | async-start | bytes 331776 | tf_op jit(solution)/shard_map/reduce_scatter | solution.py:18
  8.7 50.2 %all-gather.11.cloned.1.call-start = ((), (), s32[]{:S(2)}) async-start(), calls=%async_computation.9 | async-start | bytes 1880064 | tf_op jit(solution)/shard_map/all_gather | solution.py:25
  9.3 137.5 %all-gather.13.cloned.1.call-start = ((), (), s32[]{:S(2)}) async-start(), calls=%async_computation.11 | async-start | bytes 1880064 | tf_op jit(solution)/shard_map/all_gather | solution.py:21
  36.3 137.8 %copy-start = (bf16[144,288]{1,0:T(8,128)(2,1)S(1)}, bf16[144,288]{1,0:T(8,128)(2,1)}, u32[]{:S(2)}) copy-start(bf16[144,288]{1,0:T(8,128)(2,1)} %param.6) | copy-start | bytes 248836
  36.3 136.1 %reduce-scatter.16.cloned.1.call-start = ((), (), s32[]{:S(2)}) async-start(), calls=%async_computation.20 | async-start | bytes 663552
  150.5 90.3 %all-gather.17.cloned.1.call-start = ((), (), s32[]{:S(2)}) async-start(), calls=%async_computation.13 | async-start | bytes 1880064 | tf_op jit(solution)/shard_map/all_gather | solution.py:36
  151.1 134.9 %all-gather.15.cloned.1.call-start = ((), (), s32[]{:S(2)}) async-start(), calls=%async_computation.12 | async-start | bytes 1880064 | tf_op jit(solution)/shard_map/all_gather | solution.py:32
  174.0 203.3 %all-gather.9.cloned.1.call-start = ((), (), s32[]{:S(2)}) async-start(), calls=%async_computation.7 | async-start | bytes 1880064 | tf_op jit(solution)/shard_map/all_gather | solution.py:45
  180.9 197.9 %reduce-scatter.12.cloned.1.call-start = ((), (), s32[]{:S(2)}) async-start(), calls=%async_computation.14 | async-start | bytes 663552 | tf_op jit(solution)/shard_map/reduce_scatter | solution.py:39
  289.6 208.8 %all-reduce.3.cloned.1.call-start = ((), (), s32[]{:S(2)}) async-start(), calls=%async_computation.8 | async-start | bytes 3538944 | tf_op jit(solution)/shard_map/psum | solution.py:13
  378.7 0.9 copy-start.2
  378.7 1.0 copy-start.3
  378.7 2.9 copy-start.1
  378.7 210.9 %all-gather.19.cloned.1.call-start = ((), (), s32[]{:S(2)}) async-start(), calls=%async_computation.15 | async-start | bytes 1880064 | tf_op jit(solution)/shard_map/all_gather | solution.py:43
  381.6 252.2 %all-gather.23.cloned.1.call-start = ((), (), s32[]{:S(2)}) async-start(), calls=%async_computation.17 | async-start | bytes 1880064 | tf_op jit(solution)/shard_map/all_gather | solution.py:53
  388.4 246.9 %reduce-scatter.18.cloned.1.call-start = ((), (), s32[]{:S(2)}) async-start(), calls=%async_computation.21 | async-start | bytes 663552
  593.3 199.2 %all-reduce.5.cloned.1.call-start = ((), (), s32[]{:S(2)}) async-start(), calls=%async_computation.18 | async-start | bytes 3538944 | tf_op jit(solution)/shard_map/psum | solution.py:13
  635.2 210.7 %all-gather.21.cloned.1.call-start = ((), (), s32[]{:S(2)}) async-start(), calls=%async_computation.16 | async-start | bytes 1880064 | tf_op jit(solution)/shard_map/all_gather | solution.py:51
  636.9 233.3 %reduce-scatter.14.cloned.1.call-start = ((), (), s32[]{:S(2)}) async-start(), calls=%async_computation.19 | async-start | bytes 663552 | tf_op jit(solution)/shard_map/reduce_scatter | solution.py:58
Sparse Core Ops, SparseCore 0:
  11.6 24.5 reduce-scatter.9
  150.6 21.7 reduce-scatter.15
  289.7 20.4 reduce-scatter.11
  593.5 21.7 reduce-scatter.17
  849.7 20.4 reduce-scatter.13
Sparse Core Ops, SparseCore 1:
  11.3 47.5 all-gather.10
  62.0 84.7 all-gather.12
  154.7 86.1 all-gather.16
  243.7 42.2 all-gather.14
  289.7 87.5 all-gather.8
  379.7 118.7 all-reduce.2
  502.6 87.0 all-gather.18
  591.6 42.2 all-gather.22
  636.6 155.9 all-reduce.4
  795.5 50.3 all-gather.20
where the time goes:
time: 878 us; the launch traced here: 877 us
  waiting for transfers between devices  824 us (94%)
  between operations  15.4 us (2%)
  matrix products  14.8 us (2%)
  blocking collectives  11.5 us (1%)
    psum x2, waiting for transfers between devices, from_root(): return lax.psum(block, axis)  266 us
    all_gather x1, waiting for transfers between devices, on_device(): normed_panel = lax.all_gather(normed, 'row', axis=0, tiled=True)  91.2 us
    all_gather x1, waiting for transfers between devices, on_device(): grad_panel = lax.all_gather(grad_half, 'row', axis=0, tiled=True)  87.9 us
    all_gather x1, waiting for transfers between devices, on_device(): left_rows = lax.all_gather(left_parts, 'row', axis=1, tiled=True)  87.6 us
    all_gather x1, waiting for transfers between devices, on_device(): lax.all_gather(basis_right, 'row', axis=0, tiled=True)  59.9 us
    all_gather x1, waiting for transfers between devices, on_device(): back_panel = lax.all_gather(back_left, 'col', axis=1, tiled=True)  53.3 us
    all_gather x1, waiting for transfers between devices, on_device(): rotated_panel = lax.all_gather(rotated, 'col', axis=1, tiled=True)  45.2 us
    all_gather x1, waiting for transfers between devices, on_device(): right_rows = lax.all_gather(right_parts, 'col', axis=1, tiled=True)  40.4 us
  transfers between devices with their start and end apart: 15, of which 13 were waited for; matrix products, arithmetic and copies ran while one was open for 2% of the time, Pallas kernels for 0%

commit v1 on v0

v1 whole, which is shorter than its diff:
```python
import jax
import jax.numpy as jnp
from jax import lax
from jax.experimental import pallas as pl
from jax.experimental.pallas import tpu as pltpu
from jax.sharding import Mesh, PartitionSpec as P

BETA_ONE = 0.9
BETA_TWO = 0.95
EPSILON = 1e-08

BITS = ("xh", "z2", "z1", "z0", "y2", "y1", "y0", "core", "rep")
ROW = ("xh", "z2", "z1", "z0")
COL = ("y2", "y1", "y0", "core")
F32 = jnp.float32
BF16 = jnp.bfloat16


def move(block, swaps, flips=()):
    pairs = []
    for source in range(2 ** len(BITS)):
        bits = {name: (source >> (len(BITS) - 1 - n)) & 1 for n, name in enumerate(BITS)}
        for one, other in swaps:
            bits[one], bits[other] = bits[other], bits[one]
        for name in flips:
            bits[name] = 1 - bits[name]
        target = 0
        for name in BITS:
            target = target * 2 + bits[name]
        pairs.append((source, target))
    return lax.ppermute(block, BITS, pairs)


def call(kernel, out_shape, *operands, blocks=None):
    blocks = blocks or [None] * len(operands)
    specs = []
    for operand, block in zip(operands, blocks):
        shape, index = block or (operand.shape, (0,) * operand.ndim)
        specs.append(pl.BlockSpec(shape, lambda i, index=index: index))
    return pl.pallas_call(
        kernel,
        grid=(1,),
        out_shape=jax.ShapeDtypeStruct(out_shape, BF16),
        in_specs=specs,
        out_specs=pl.BlockSpec(out_shape, lambda i: (0,) * len(out_shape)),
        compiler_params=pltpu.CompilerParams(vmem_limit_bytes=32 * 2**20),
    )(*operands)


def first_kernel(left_ref, grad_ref, out_ref):
    for block in range(2):
        total = None
        for k in range(8):
            part = lax.dot_general(
                left_ref[k // 4, block, k % 4, 0], grad_ref[k], (((0,), (0,)), ((), ())),
                preferred_element_type=F32,
            )
            total = part if total is None else total + part
        out_ref[block] = total.astype(BF16)


def second_kernel(rotated_ref, right_ref, out_ref):
    for column in range(2):
        total = None
        for k in range(8):
            part = jnp.dot(
                rotated_ref[k], right_ref[k, column], preferred_element_type=F32
            )
            total = part if total is None else total + part
        out_ref[column] = total.astype(BF16)


def third_kernel(left_ref, normed_ref, out_ref):
    for block in range(4):
        total = None
        for k in range(4):
            part = jnp.dot(
                left_ref[k // 2, block, k % 2, 0], normed_ref[k], preferred_element_type=F32
            )
            total = part if total is None else total + part
        out_ref[block] = total.astype(BF16)


def fourth_kernel(back_ref, right_ref, out_ref):
    for column in range(2):
        total = None
        for k in range(8):
            part = lax.dot_general(
                back_ref[k], right_ref[k, column], (((1,), (1,)), ((), ())),
                preferred_element_type=F32,
            )
            total = part if total is None else total + part
        out_ref[column] = total.astype(BF16)


def exchange(parts, axes):
    return jnp.sum(lax.all_to_all(parts, axes, 0, 0).astype(F32), axis=0)


def spread(block, axes):
    copies = 2 ** len(axes)
    return lax.all_to_all(jnp.broadcast_to(block[None], (copies,) + block.shape), axes, 0, 0)


def on_device(grad_parts, basis_left, basis_right, first_moment, second_moment):
    half = basis_left.shape[0]
    width = basis_left.shape[1]
    grad = grad_parts[0]
    rep = lax.axis_index("rep")

    left = jnp.concatenate(
        [
            move(basis_left, [("z2", "y1")]),
            move(basis_left, [("xh", "y2"), ("z0", "core")]),
        ]
    )
    left = lax.all_gather(left, ("y2", "y1", "y0", "core"))

    own = lax.dynamic_slice_in_dim(grad, rep * half, half, 0)
    other = lax.dynamic_slice_in_dim(grad, (1 - rep) * half, half, 0)
    grad_half = (own.astype(F32) + move(other, [], ["rep"]).astype(F32)).astype(BF16)
    grad_panel = spread(grad_half, ("xh", "z1", "z0"))

    right = jnp.concatenate(
        [
            move(basis_right, [("xh", "y2")]),
            move(basis_right, [("z2", "y1"), ("z1", "y0"), ("z0", "core")]),
        ]
    )
    right = lax.all_gather(right, ("xh", "rep"))
    right_second = lax.all_gather(right[:, :half], ("z2", "z1", "z0"))
    right_second = right_second.reshape(8, 2, width, width)

    parts = call(
        first_kernel, (2, width, width),
        left.reshape(2, 2, 4, 2, half, width), grad_panel,
        blocks=[((2, 2, 4, 1, half, width), (0, 0, 0, 0, 0, 0)), None],
    )
    rotated = exchange(parts.reshape(4, half, width), ("z2", "rep")).astype(BF16)
    rotated, right = lax.optimization_barrier((rotated, right))
    right_fourth = lax.all_gather(right[:, half:], ("z2", "z1", "z0"))
    right_fourth = right_fourth.reshape(8, 2, width, width)
    rotated_panel = lax.all_gather(rotated, ("y1", "y0", "core"))

    parts = call(second_kernel, (2, half, width), rotated_panel, right_second)
    projected = exchange(parts, ("y2",))

    new_first = BETA_ONE * first_moment + (1.0 - BETA_ONE) * projected
    new_second = BETA_TWO * second_moment + (1.0 - BETA_TWO) * projected * projected
    normed = (new_first / (jnp.sqrt(new_second) + EPSILON)).astype(BF16)
    normed_panel = spread(normed, ("xh", "z0", "rep")).reshape(4, width, width)

    parts = call(
        third_kernel, (4, half, width),
        left.reshape(2, 4, 2, 2, half, width), normed_panel,
        blocks=[((2, 4, 2, 1, half, width), (0, 0, 0, 1, 0, 0)), None],
    )
    back_left = exchange(parts, ("z2", "z1")).astype(BF16)
    back_panel = lax.all_gather(back_left, ("y1", "y0", "core"))

    parts = call(fourth_kernel, (2, half, width), back_panel, right_fourth)
    update = exchange(parts, ("y2",))
    return (update, new_first, new_second)


def solution(mesh):
    bits = Mesh(mesh.devices.reshape((2,) * len(BITS)), BITS)
    block = P(ROW + ("rep",), COL)
    in_specs = (P("rep", ROW, COL), P(COL + ("rep",), ROW), block, block, block)
    return jax.shard_map(
        on_device, mesh=bits, in_specs=in_specs, out_specs=(block,) * 3, check_vma=False
    )
```

time: 878 us -> 259 us (0.29)
  waiting for transfers between devices: 824 us -> 9.14 us
  blocking collectives: 11.5 us -> 203 us
  matrix products: 14.8 us -> 0 us
  starting transfers between devices: 0.63 us -> 15.4 us
    all_gather x8 -> x3, waiting for transfers between devices: 488 us -> 0.01 us  [the longest x1 0.01 us: on_device(): left = lax.all_gather(left, ('y2', 'y1', 'y0', 'core'))]
    psum x2 -> x0, waiting for transfers between devices: 266 us -> none  [from_root(): return lax.psum(block, axis)]
    all_to_all x2 -> x6, blocking collectives: 11.5 us -> 126 us  [the longest x4 69.8 us: exchange(): return jnp.sum(lax.all_to_all(parts, axes, 0, 0).astype(F32), axis=0)]
    all_gather x0 -> x3, blocking collectives: none -> 76.8 us  [the longest x1 28.5 us: on_device(): rotated_panel = lax.all_gather(rotated, ('y1', 'y0', 'core'))]
    reduce_scatter x3 -> x0, waiting for transfers between devices: 47.5 us -> none  [the longest x1 26.9 us: on_device(): lax.psum_scatter(grad_tile.astype(jnp.bfloat16), 'rep', scatter_dimension...]
    unnamed x17 -> x3, waiting for transfers between devices: 23.2 us -> 0.05 us
    ppermute x0 -> x5, starting transfers between devices: none -> 15.3 us  [move(): return lax.ppermute(block, BITS, pairs)]
    ppermute x0 -> x5, waiting for transfers between devices: none -> 9.09 us  [move(): return lax.ppermute(block, BITS, pairs)]
  transfers between devices with their start and end apart: 15 -> 8, of which waited for: 13 -> 3; matrix products, arithmetic and copies ran while one was open for 2% -> 1% of each run, Pallas kernels for 0% -> 2%
where the time goes in v1:
time: 259 us; the launch traced here: 258 us
  blocking collectives  203 us (78%)
  starting transfers between devices  15.4 us (6%)
  between operations  13.9 us (5%)
  waiting for transfers between devices  9.14 us (4%)
  local copies, waits for them, and re-layouts  8.07 us (3%)
  Pallas kernels  5.96 us (2%)
    all_to_all x4, blocking collectives, exchange(): return jnp.sum(lax.all_to_all(parts, axes, 0, 0).astype(F32), axis=0)  69.8 us
    all_to_all x2, blocking collectives, spread(): lax.all_to_all(jnp.broadcast_to(block[None], (copies,) + block.shape), ax...  56.3 us
    all_gather x1, blocking collectives, on_device(): rotated_panel = lax.all_gather(rotated, ('y1', 'y0', 'core'))  28.5 us
    all_gather x1, blocking collectives, on_device(): right = lax.all_gather(right, ('xh', 'rep'))  26.3 us
    all_gather x1, blocking collectives, on_device(): back_panel = lax.all_gather(back_left, ('y1', 'y0', 'core'))  22 us
    ppermute x5, starting transfers between devices, move(): return lax.ppermute(block, BITS, pairs)  15.3 us
    ppermute x5, waiting for transfers between devices, move(): return lax.ppermute(block, BITS, pairs)  9.09 us
    unnamed x14, local copies, waits for them, and re-layouts  6.27 us
  transfers between devices with their start and end apart: 8, of which 3 were waited for; matrix products, arithmetic and copies ran while one was open for 1% of the time, Pallas kernels for 2%

profile of v1, /device:TPU:1, one launch (start us, length us, event | category | flops | bytes accessed | tf_op | source)
XLA Modules:
  0.0 257.9 jit_solution(15401866267815708559)
XLA Ops:
  7.2 0.0 copy-start.6
  7.2 0.0 all-gather.10.cloned.1.call-start
  7.2 1.7 collective-permute-start
  8.9 5.4 %collective-permute-start.1 = (bf16[144,288]{1,0:T(8,128)(2,1)}, bf16[144,288]{1,0:T(8,128)(2,1)S(1)}, u32[]{:S(2)}, u32[]{:S(2)}) collective-permute-start(bf16[144,288]{1,0:T(8,128)(2,1)} %param.6), channel_id=1, source_target_pairs={{0,0},{1,1},{2,32},{3,33},{4,4},{5,5},{6,36},{7,37},{8,8},{9,9},{1... | collective-permute-start | bytes 248840 | tf_op jit(solution)/shard_map/ppermute | solution.py:31
  14.3 0.0 collective-permute-done
  14.3 2.6 %collective-permute-done.1 = bf16[144,288]{1,0:T(8,128)(2,1)S(1)} collective-permute-done((bf16[144,288]{1,0:T(8,128)(2,1)}, bf16[144,288]{1,0:T(8,128)(2,1)S(1)}, u32[]{:S(2)}, u32[]{:S(2)}) %collective-permute-start.1) | collective-permute-done | bytes 82976 | tf_op jit(solution)/shard_map/ppermute | solution.py:31
  16.9 0.7 pad_maximum_fusion
  17.6 0.0 all-gather.10.cloned.1.call-update
  17.7 0.0 all-gather.12.cloned.1.call-start
  17.7 1.6 collective-permute-start.3
  19.3 3.6 %collective-permute-start.4 = (bf16[144,288]{1,0:T(8,128)(2,1)}, bf16[144,288]{1,0:T(8,128)(2,1)S(1)}, u32[]{:S(2)}, u32[]{:S(2)}) collective-permute-start(bf16[144,288]{1,0:T(8,128)(2,1)} %param.7), channel_id=1, source_target_pairs={{0,0},{1,1},{2,32},{3,33},{4,64},{5,65},{6,96},{7,97},{8,128},{9,1... | collective-permute-start | bytes 248840 | tf_op jit(solution)/shard_map/ppermute | solution.py:31
  22.9 0.0 collective-permute-done.3
  22.9 3.7 %collective-permute-done.4 = bf16[144,288]{1,0:T(8,128)(2,1)S(1)} collective-permute-done((bf16[144,288]{1,0:T(8,128)(2,1)}, bf16[144,288]{1,0:T(8,128)(2,1)S(1)}, u32[]{:S(2)}, u32[]{:S(2)}) %collective-permute-start.4) | collective-permute-done | bytes 82976 | tf_op jit(solution)/shard_map/ppermute | solution.py:31
  26.7 26.3 %all-gather.1 = bf16[1152,288]{1,0:T(8,128)(2,1)S(1)} all-gather(bf16[288,288]{1,0:T(8,128)(2,1)S(1)} %pad_maximum_fusion.1), channel_id=3, replica_groups=mesh['xh'=2,'z2'=2,'z1'=2,'z0'=2,'y2'=2,'y1'=2,'y0'=2,'core'=2,'rep'=2] ..., dimensions={0}, use_global_device_ids=true | all-gather | bytes 829440 | tf_op jit(solution)/shard_map/all_gather | solution.py:130
  53.0 0.8 slice.8
  53.8 0.0 all-gather.12.cloned.1.call-update
  53.8 0.0 all-gather.14.cloned.1.call-start
  53.9 0.0 copy-done.6
  53.9 3.0 %collective-permute-start.2 = (bf16[144,288]{1,0:T(8,128)(2,1)S(1)}, bf16[144,288]{1,0:T(8,128)(2,1)S(1)}, u32[]{:S(2)}, u32[]{:S(2)}) collective-permute-start(bf16[144,288]{1,0:T(8,128)(2,1)S(1)} %dynamic-slice_bitcast_fusion), channel_id=1, source_target_pairs={{0,1},{1,0},{2,3},{3,2},{4,5},{5,4},{6,7},{7,6},{8,9},{9,8},{10,11... | collective-permute-start | bytes 248840 | tf_op jit(solution)/shard_map/ppermute | solution.py:31
  57.0 2.7 %collective-permute-done.2 = bf16[144,288]{1,0:T(8,128)(2,1)S(1)} collective-permute-done((bf16[144,288]{1,0:T(8,128)(2,1)S(1)}, bf16[144,288]{1,0:T(8,128)(2,1)S(1)}, u32[]{:S(2)}, u32[]{:S(2)}) %collective-permute-start.2) | collective-permute-done | bytes 82976 | tf_op jit(solution)/shard_map/ppermute | solution.py:31
  59.7 0.1 broadcast_in_dim.4
  59.8 31.0 %all_to_all.30.grad_ref = bf16[8,144,288]{2,1,0:T(8,128)(2,1)S(1)} all-to-all(bf16[8,144,288]{2,1,0:T(8,128)(2,1)S(1)} %broadcast_in_dim.4), channel_id=1, replica_groups=mesh['xh'=2,'z2'=2,'z1'=2,'z0'=2,'y2'=2,'y1'=2,'y0'=2,'core'=2,'rep'=2] ..., dimensions={0} | all-to-all | bytes 1327104 | tf_op jit(solution)/shard_map/all_to_all | solution.py:102
  90.9 0.0 all-gather.10.cloned.1.call-done
  90.9 0.0 copy-start
  90.9 2.1 copy-done
  93.0 1.6 shard_map.76
  94.5 32.4 %all_to_all.31 = bf16[4,144,288]{2,1,0:T(8,128)(2,1)S(1)} all-to-all(bf16[4,144,288]{2,1,0:T(8,128)(2,1)S(1)} %bitcast.21), channel_id=1, replica_groups=mesh['xh'=2,'z2'=2,'z1'=2,'z0'=2,'y2'=2,'y1'=2,'y0'=2,'core'=2,'rep'=2] ..., dimensions={0} | all-to-all | bytes 663552 | tf_op jit(solution)/shard_map/all_to_all | solution.py:97
  127.0 0.1 reduce_sum.42
  127.0 0.8 slice.7
  127.8 0.0 copy-start.4
  127.9 0.0 copy-start.5
  127.9 0.0 all-gather.14.cloned.1.call-update
  127.9 28.5 %all-gather.2 = bf16[1152,288]{1,0:T(8,128)(2,1)S(1)} all-gather(bf16[144,288]{1,0:T(8,128)(2,1)S(1)} %reduce_sum.42), channel_id=4, replica_groups=mesh['xh'=2,'z2'=2,'z1'=2,'z0'=2,'y2'=2,'y1'=2,'y0'=2,'core'=2,'rep'=2] ..., dimensions={0}, use_global_device_ids=true | all-gather | bytes 746496 | tf_op jit(solution)/shard_map/all_gather | solution.py:143
  156.4 0.0 all-gather.12.cloned.1.call-done
  156.4 0.0 copy-start.2
  156.4 2.2 copy-done.2
  158.5 1.4 shard_map.77
  159.9 0.0 copy-start.1
  159.9 11.4 %all_to_all.32 = bf16[2,144,288]{2,1,0:T(8,128)(2,1)S(1)} all-to-all(bf16[2,144,288]{2,1,0:T(8,128)(2,1)S(1)} %shard_map.77), channel_id=1, replica_groups=mesh['xh'=2,'z2'=2,'z1'=2,'z0'=2,'y2'=2,'y1'=2,'y0'=2,'core'=2,'rep'=2] ..., dimensions={0} | all-to-all | bytes 331776 | tf_op jit(solution)/shard_map/all_to_all | solution.py:97
  171.4 0.0 copy-done.4
  171.4 0.0 copy-done.5
  171.4 0.9 divide_convert_fusion
  172.3 0.1 broadcast_in_dim.5
  172.4 25.3 %all_to_all.33 = bf16[8,144,288]{2,1,0:T(8,128)(2,1)S(1)} all-to-all(bf16[8,144,288]{2,1,0:T(8,128)(2,1)S(1)} %broadcast_in_dim.5), channel_id=1, replica_groups=mesh['xh'=2,'z2'=2,'z1'=2,'z0'=2,'y2'=2,'y1'=2,'y0'=2,'core'=2,'rep'=2] ..., dimensions={0} | all-to-all | bytes 1327104 | tf_op jit(solution)/shard_map/all_to_all | solution.py:102
  197.6 0.0 copy-done.1
  197.6 1.4 shard_map.78
  199.0 13.0 %all_to_all.34 = bf16[4,144,288]{2,1,0:T(8,128)(2,1)S(1)} all-to-all(bf16[4,144,288]{2,1,0:T(8,128)(2,1)S(1)} %shard_map.78), channel_id=1, replica_groups=mesh['xh'=2,'z2'=2,'z1'=2,'z0'=2,'y2'=2,'y1'=2,'y0'=2,'core'=2,'rep'=2] ..., dimensions={0} | all-to-all | bytes 663552 | tf_op jit(solution)/shard_map/all_to_all | solution.py:97
  212.0 0.1 reduce_sum.44
  212.1 22.0 %all-gather.4 = bf16[1152,288]{1,0:T(8,128)(2,1)S(1)} all-gather(bf16[144,288]{1,0:T(8,128)(2,1)S(1)} %reduce_sum.44), channel_id=6, replica_groups=mesh['xh'=2,'z2'=2,'z1'=2,'z0'=2,'y2'=2,'y1'=2,'y0'=2,'core'=2,'rep'=2] ..., dimensions={0}, use_global_device_ids=true | all-gather | bytes 746496 | tf_op jit(solution)/shard_map/all_gather | solution.py:159
  234.0 0.0 all-gather.14.cloned.1.call-done
  234.1 0.0 copy-start.3
  234.1 2.0 copy-done.3
  236.1 1.6 shard_map.79
  237.7 13.0 %all_to_all.35 = bf16[2,144,288]{2,1,0:T(8,128)(2,1)S(1)} all-to-all(bf16[2,144,288]{2,1,0:T(8,128)(2,1)S(1)} %shard_map.79), channel_id=1, replica_groups=mesh['xh'=2,'z2'=2,'z1'=2,'z0'=2,'y2'=2,'y1'=2,'y0'=2,'core'=2,'rep'=2] ..., dimensions={0} | all-to-all | bytes 331776 | tf_op jit(solution)/shard_map/all_to_all | solution.py:97
  250.7 0.7 convert_reduce_fusion
  (4 shorter events, 0.1 us)
Async XLA Ops:
  7.2 46.7 %copy-start.6 = (bf16[1,288,288]{2,1,0:T(8,128)(2,1)S(1)}, bf16[1,288,288]{2,1,0:T(8,128)(2,1)}, u32[]{:S(2)}) copy-start(bf16[1,288,288]{2,1,0:T(8,128)(2,1)} %param.5) | copy-start | bytes 497668
  7.2 83.7 %all-gather.10.cloned.1.call-start = ((), (), s32[]{:S(2)}) async-start(), calls=%async_computation.6 | async-start | bytes 3760128 | tf_op jit(solution)/shard_map/all_gather | solution.py:117
  7.2 7.1 %collective-permute-start = (bf16[144,288]{1,0:T(8,128)(2,1)}, bf16[144,288]{1,0:T(8,128)(2,1)S(1)}, u32[]{:S(2)}, u32[]{:S(2)}) collective-permute-start(bf16[144,288]{1,0:T(8,128)(2,1)} %param.6), channel_id=1, source_target_pairs={{0,0},{1,1},{2,2},{3,3},{4,4},{5,5},{6,6},{7,7},{8,128},{9,129},{1... | collective-permute-start | bytes 248840 | tf_op jit(solution)/shard_map/ppermute | solution.py:31
  8.9 8.0 %collective-permute-start.1 = (bf16[144,288]{1,0:T(8,128)(2,1)}, bf16[144,288]{1,0:T(8,128)(2,1)S(1)}, u32[]{:S(2)}, u32[]{:S(2)}) collective-permute-start(bf16[144,288]{1,0:T(8,128)(2,1)} %param.6), channel_id=1, source_target_pairs={{0,0},{1,1},{2,32},{3,33},{4,4},{5,5},{6,36},{7,37},{8,8},{9,9},{1... | collective-permute-start | bytes 248840 | tf_op jit(solution)/shard_map/ppermute | solution.py:31
  17.7 138.7 %all-gather.12.cloned.1.call-start = ((), (), s32[]{:S(2)}) async-start(), calls=%async_computation.7 | async-start | bytes 3981312 | tf_op jit(solution)/shard_map/all_gather | solution.py:131
  17.7 5.2 %collective-permute-start.3 = (bf16[144,288]{1,0:T(8,128)(2,1)}, bf16[144,288]{1,0:T(8,128)(2,1)S(1)}, u32[]{:S(2)}, u32[]{:S(2)}) collective-permute-start(bf16[144,288]{1,0:T(8,128)(2,1)} %param.7), channel_id=1, source_target_pairs={{0,0},{1,1},{2,2},{3,3},{4,4},{5,5},{6,6},{7,7},{8,8},{9,9},{10,10... | collective-permute-start | bytes 248840 | tf_op jit(solution)/shard_map/ppermute | solution.py:31
  19.3 7.4 %collective-permute-start.4 = (bf16[144,288]{1,0:T(8,128)(2,1)}, bf16[144,288]{1,0:T(8,128)(2,1)S(1)}, u32[]{:S(2)}, u32[]{:S(2)}) collective-permute-start(bf16[144,288]{1,0:T(8,128)(2,1)} %param.7), channel_id=1, source_target_pairs={{0,0},{1,1},{2,32},{3,33},{4,64},{5,65},{6,96},{7,97},{8,128},{9,1... | collective-permute-start | bytes 248840 | tf_op jit(solution)/shard_map/ppermute | solution.py:31
  53.8 180.2 %all-gather.14.cloned.1.call-start = ((), (), s32[]{:S(2)}) async-start(), calls=%async_computation.8 | async-start | bytes 3981312 | tf_op jit(solution)/shard_map/all_gather | solution.py:141
  53.9 5.8 %collective-permute-start.2 = (bf16[144,288]{1,0:T(8,128)(2,1)S(1)}, bf16[144,288]{1,0:T(8,128)(2,1)S(1)}, u32[]{:S(2)}, u32[]{:S(2)}) collective-permute-start(bf16[144,288]{1,0:T(8,128)(2,1)S(1)} %dynamic-slice_bitcast_fusion), channel_id=1, source_target_pairs={{0,1},{1,0},{2,3},{3,2},{4,5},{5,4},{6,7},{7,6},{8,9},{9,8},{10,11... | collective-permute-start | bytes 248840 | tf_op jit(solution)/shard_map/ppermute | solution.py:31
  90.9 2.1 copy-start
  127.8 43.5 %copy-start.4 = (f32[144,288]{1,0:T(8,128)S(1)}, f32[144,288]{1,0:T(8,128)}, u32[]{:S(2)}) copy-start(f32[144,288]{1,0:T(8,128)} %param.9) | copy-start | bytes 497668
  127.9 43.5 %copy-start.5 = (f32[144,288]{1,0:T(8,128)S(1)}, f32[144,288]{1,0:T(8,128)}, u32[]{:S(2)}) copy-start(f32[144,288]{1,0:T(8,128)} %param.8) | copy-start | bytes 497668
  156.4 2.2 copy-start.2
  159.9 37.7 %copy-start.1 = (bf16[4608,288]{1,0:T(8,128)(2,1)S(1)}, bf16[4608,288]{1,0:T(8,128)(2,1)}, u32[]{:S(2)}) copy-start(bf16[4608,288]{1,0:T(8,128)(2,1)} %all-gather.10.cloned.1.call-done) | copy-start | bytes 7962628
  234.1 2.0 copy-start.3
Sparse Core Ops, SparseCore 0:
  17.8 60.7 all-gather.9
  80.7 63.6 all-gather.11
  146.4 57.3 all-gather.13

commit v2 on v1

v2 whole, which is shorter than its diff:
```python
import jax
import jax.numpy as jnp
from jax import lax
from jax.experimental import pallas as pl
from jax.experimental.pallas import tpu as pltpu
from jax.sharding import Mesh, PartitionSpec as P

BETA_ONE = 0.9
BETA_TWO = 0.95
EPSILON = 1e-08

BITS = ("xh", "z2", "z1", "z0", "y2", "y1", "y0", "core", "rep")
ROW = ("xh", "z2", "z1", "z0")
COL = ("y2", "y1", "y0", "core")
F32 = jnp.float32
BF16 = jnp.bfloat16


def move(block, swaps, flips=()):
    pairs = []
    for source in range(2 ** len(BITS)):
        bits = {name: (source >> (len(BITS) - 1 - n)) & 1 for n, name in enumerate(BITS)}
        for one, other in swaps:
            bits[one], bits[other] = bits[other], bits[one]
        for name in flips:
            bits[name] = 1 - bits[name]
        target = 0
        for name in BITS:
            target = target * 2 + bits[name]
        pairs.append((source, target))
    return lax.ppermute(block, BITS, pairs)


def call(kernel, out_shape, *operands):
    return pl.pallas_call(
        kernel,
        out_shape=jax.ShapeDtypeStruct(out_shape, BF16),
        in_specs=[pl.BlockSpec(memory_space=pltpu.VMEM)] * len(operands),
        out_specs=pl.BlockSpec(memory_space=pltpu.VMEM),
        compiler_params=pltpu.CompilerParams(vmem_limit_bytes=32 * 2**20),
    )(*operands)


def first_kernel(left_ref, grad_ref, out_ref):
    for block in range(4):
        total = None
        for k in range(4):
            part = lax.dot_general(
                left_ref[block // 2, k, block % 2], grad_ref[k], (((0,), (0,)), ((), ())),
                preferred_element_type=F32,
            )
            total = part if total is None else total + part
        out_ref[block] = total.astype(BF16)


def second_kernel(rotated_ref, right_ref, out_ref):
    for block in range(4):
        total = None
        for k in range(4):
            part = jnp.dot(
                rotated_ref[k], right_ref[block % 2, k, block // 2],
                preferred_element_type=F32,
            )
            total = part if total is None else total + part
        out_ref[block] = total.astype(BF16)


def third_kernel(left_ref, normed_ref, out_ref):
    for block in range(4):
        total = None
        for k in range(4):
            part = jnp.dot(
                left_ref[k // 2, block, k % 2], normed_ref[k], preferred_element_type=F32
            )
            total = part if total is None else total + part
        out_ref[block] = total.astype(BF16)


def fourth_kernel(back_ref, right_ref, out_ref):
    for block in range(4):
        total = None
        for k in range(4):
            part = lax.dot_general(
                back_ref[k], right_ref[k % 2, block, k // 2], (((1,), (1,)), ((), ())),
                preferred_element_type=F32,
            )
            total = part if total is None else total + part
        out_ref[block] = total.astype(BF16)


def exchange(parts, axes):
    return jnp.sum(lax.all_to_all(parts, axes, 0, 0).astype(F32), axis=0)


def spread(block, axes):
    copies = 2 ** len(axes)
    return lax.all_to_all(jnp.broadcast_to(block[None], (copies,) + block.shape), axes, 0, 0)


def on_device(grad_parts, basis_left, basis_right, first_moment, second_moment):
    half = basis_left.shape[0]
    width = basis_left.shape[1]
    grad = grad_parts[0]
    rep = lax.axis_index("rep")

    left = move(basis_left, [("xh", "y2"), ("z0", "core")])
    left = lax.all_gather(left, ("y2", "y1", "y0", "core"))
    left = left.reshape(2, 4, 2, half, width)

    right = move(basis_right, [("xh", "y2"), ("z2", "y1")])
    right = lax.all_gather(right, ("xh", "rep"))
    right = lax.all_gather(right, ("z2", "z1", "z0"))
    right = right.reshape(2, 4, 2, width, width)

    own = lax.dynamic_slice_in_dim(grad, rep * half, half, 0)
    other = lax.dynamic_slice_in_dim(grad, (1 - rep) * half, half, 0)
    grad_half = (own.astype(F32) + move(other, [], ["rep"]).astype(F32)).astype(BF16)

    grad_panel = spread(grad_half, ("z2", "z1"))
    parts = call(first_kernel, (4, width, width), left, grad_panel)
    parts = parts.reshape(8, half, width)
    rotated = exchange(parts, ("xh", "z0", "rep")).astype(BF16)

    rotated_panel = lax.all_gather(rotated, ("y0", "core"))
    parts = call(second_kernel, (4, half, width), rotated_panel, right)
    projected = exchange(parts, ("y2", "y1"))

    new_first = BETA_ONE * first_moment + (1.0 - BETA_ONE) * projected
    new_second = BETA_TWO * second_moment + (1.0 - BETA_TWO) * projected * projected
    normed = (new_first / (jnp.sqrt(new_second) + EPSILON)).astype(BF16)

    normed_panel = spread(normed, ("xh", "z0", "rep")).reshape(4, width, width)
    parts = call(third_kernel, (4, half, width), left, normed_panel)
    back_left = exchange(parts, ("z2", "z1")).astype(BF16)

    back_panel = lax.all_gather(back_left, ("y2", "y1"))
    parts = call(fourth_kernel, (4, half, width), back_panel, right)
    update = exchange(parts, ("y0", "core"))
    return (update, new_first, new_second)


def solution(mesh):
    bits = Mesh(mesh.devices.reshape((2,) * len(BITS)), BITS)
    block = P(ROW + ("rep",), COL)
    in_specs = (P("rep", ROW, COL), P(COL + ("rep",), ROW), block, block, block)
    return jax.shard_map(
        on_device, mesh=bits, in_specs=in_specs, out_specs=(block,) * 3, check_vma=False
    )
```

time: 259 us -> 230 us (0.89)
  blocking collectives: 203 us -> 180 us
  starting transfers between devices: 15.4 us -> 9.3 us
  local copies, waits for them, and re-layouts: 8.07 us -> 5.17 us
    all_to_all x2, blocking collectives: 56.3 us -> 38.1 us  [spread(): lax.all_to_all(jnp.broadcast_to(block[None], (copies,) + block.shape), ax...]
    all_gather x2, blocking collectives: 50.5 us -> 34.9 us  [the longest x1 18.6 us: on_device(): rotated_panel = lax.all_gather(rotated, ('y0', 'core'))]
    all_to_all x4, blocking collectives: 69.8 us -> 76.7 us  [exchange(): return jnp.sum(lax.all_to_all(parts, axes, 0, 0).astype(F32), axis=0)]
    ppermute x5 -> x3, starting transfers between devices: 15.3 us -> 9.22 us  [move(): return lax.ppermute(block, BITS, pairs)]
    all_gather x2 -> x1, waiting for transfers between devices: 0.01 us -> 4.94 us  [on_device(): right = lax.all_gather(right, ('z2', 'z1', 'z0'))]
    all_gather x1, blocking collectives: 26.3 us -> 30.4 us  [on_device(): right = lax.all_gather(right, ('xh', 'rep'))]
    ppermute x5 -> x3, waiting for transfers between devices: 9.09 us -> 5.85 us  [move(): return lax.ppermute(block, BITS, pairs)]
  transfers between devices with their start and end apart: 8 -> 5, of which waited for: 3 -> 3; matrix products, arithmetic and copies ran while one was open for 1% -> 1% of each run, Pallas kernels for 2% -> 1%
where the time goes in v2:
time: 230 us
  blocking collectives  180 us (78%)
  between operations  14.2 us (6%)
  waiting for transfers between devices  10.8 us (5%)
  starting transfers between devices  9.3 us (4%)
  Pallas kernels  5.83 us (3%)
  local copies, waits for them, and re-layouts  5.17 us (2%)
  other arithmetic  4.53 us (2%)
    all_to_all x4, blocking collectives, exchange(): return jnp.sum(lax.all_to_all(parts, axes, 0, 0).astype(F32), axis=0)  76.7 us
    all_to_all x2, blocking collectives, spread(): lax.all_to_all(jnp.broadcast_to(block[None], (copies,) + block.shape), ax...  38.1 us
    all_gather x1, blocking collectives, on_device(): right = lax.all_gather(right, ('xh', 'rep'))  30.4 us
    all_gather x1, blocking collectives, on_device(): rotated_panel = lax.all_gather(rotated, ('y0', 'core'))  18.6 us
    all_gather x1, blocking collectives, on_device(): back_panel = lax.all_gather(back_left, ('y2', 'y1'))  16.3 us
    ppermute x3, starting transfers between devices, move(): return lax.ppermute(block, BITS, pairs)  9.22 us
    ppermute x3, waiting for transfers between devices, move(): return lax.ppermute(block, BITS, pairs)  5.85 us
    pallas_call x4, Pallas kernels, call(): pl.pallas_call(kernel, out_shape=jax.ShapeDtypeStruct(out_shape, BF16), i...  5.83 us
  transfers between devices with their start and end apart: 5, of which 3 were waited for; matrix products, arithmetic and copies ran while one was open for 1% of the time, Pallas kernels for 1%

profile of v2, /device:TPU:1, one launch (start us, length us, event | category | flops | bytes accessed | tf_op | source)
XLA Modules:
  0.0 229.8 jit_solution(3511754558307960752)
XLA Ops:
  7.2 0.0 all-gather.8.cloned.1.call-start
  7.2 5.4 %collective-permute-start = (bf16[144,288]{1,0:T(8,128)(2,1)}, bf16[144,288]{1,0:T(8,128)(2,1)S(1)}, u32[]{:S(2)}, u32[]{:S(2)}) collective-permute-start(bf16[144,288]{1,0:T(8,128)(2,1)} %param.6), channel_id=1, source_target_pairs={{0,0},{1,1},{2,32},{3,33},{4,4},{5,5},{6,36},{7,37},{8,8},{9,9},{1... | collective-permute-start | bytes 248840 | tf_op jit(solution)/shard_map/ppermute | solution.py:31
  12.6 2.6 %collective-permute-done = bf16[144,288]{1,0:T(8,128)(2,1)S(1)} collective-permute-done((bf16[144,288]{1,0:T(8,128)(2,1)}, bf16[144,288]{1,0:T(8,128)(2,1)S(1)}, u32[]{:S(2)}, u32[]{:S(2)}) %collective-permute-start) | collective-permute-done | bytes 82976 | tf_op jit(solution)/shard_map/ppermute | solution.py:31
  15.2 0.0 copy-start.6
  15.2 0.6 copy-done.6
  15.9 0.0 all-gather.8.cloned.1.call-update
  15.9 0.0 all-gather.10.cloned.1.call-start
  16.0 1.6 collective-permute-start.2
  17.5 0.0 collective-permute-done.2
  17.5 30.4 %all-gather.2 = bf16[576,288]{1,0:T(8,128)(2,1)} all-gather(bf16[144,288]{1,0:T(8,128)(2,1)S(1)} %collective-permute-done.2), channel_id=4, replica_groups=mesh['xh'=2,'z2'=2,'z1'=2,'z0'=2,'y2'=2,'y1'=2,'y0'=2,'core'=2,'rep'=2] ..., dimensions={0}, use_global_device_ids=true | all-gather | bytes 414720 | tf_op jit(solution)/shard_map/all_gather | solution.py:111
  47.9 0.0 all-gather.10.cloned.1.call-update
  47.9 0.9 dynamic-slice_bitcast_fusion
  48.8 2.3 collective-permute-start.1
  51.1 3.2 %collective-permute-done.1 = bf16[144,288]{1,0:T(8,128)(2,1)S(1)} collective-permute-done((bf16[144,288]{1,0:T(8,128)(2,1)S(1)}, bf16[144,288]{1,0:T(8,128)(2,1)S(1)}, u32[]{:S(2)}, u32[]{:S(2)}) %collective-permute-start.1) | collective-permute-done | bytes 82976 | tf_op jit(solution)/shard_map/ppermute | solution.py:31
  54.3 0.9 fusion.1
  55.3 23.5 %all_to_all.30.grad_ref = bf16[4,144,288]{2,1,0:T(8,128)(2,1)S(1)} all-to-all(bf16[4,144,288]{2,1,0:T(8,128)(2,1)S(1)} %broadcast_in_dim.4), channel_id=1, replica_groups=mesh['xh'=2,'z2'=2,'z1'=2,'z0'=2,'y2'=2,'y1'=2,'y0'=2,'core'=2,'rep'=2] ..., dimensions={0} | all-to-all | bytes 663552 | tf_op jit(solution)/shard_map/all_to_all | solution.py:97
  78.8 0.0 all-gather.8.cloned.1.call-done
  78.8 0.0 copy-start.2
  78.8 1.5 copy-done.2
  80.2 1.4 shard_map.76
  81.7 24.8 %all_to_all.31 = bf16[8,144,288]{2,1,0:T(8,128)(2,1)S(1)} all-to-all(bf16[8,144,288]{2,1,0:T(8,128)(2,1)S(1)} %bitcast.17), channel_id=1, replica_groups=mesh['xh'=2,'z2'=2,'z1'=2,'z0'=2,'y2'=2,'y1'=2,'y0'=2,'core'=2,'rep'=2] ..., dimensions={0} | all-to-all | bytes 1327104 | tf_op jit(solution)/shard_map/all_to_all | solution.py:92
  106.5 0.0 copy-start.4
  106.5 0.0 copy-start.5
  106.5 0.1 reduce_sum.42
  106.6 18.6 %all-gather.1 = bf16[576,288]{1,0:T(8,128)(2,1)S(1)} all-gather(bf16[144,288]{1,0:T(8,128)(2,1)S(1)} %reduce_sum.42), channel_id=3, replica_groups=mesh['xh'=2,'z2'=2,'z1'=2,'z0'=2,'y2'=2,'y1'=2,'y0'=2,'core'=2,'rep'=2] ..., dimensions={0}, use_global_device_ids=true | all-gather | bytes 414720 | tf_op jit(solution)/shard_map/all_gather | solution.py:124
  125.2 4.9 %all-gather.10.cloned.1.call-done = bf16[32,144,288]{2,1,0:T(8,128)(2,1)} async-done(((bf16[4,144,288]{2,1,0:T(8,128)(2,1)}), bf16[32,144,288]{2,1,0:T(8,128)(2,1)}) %all-gather.10.cloned.1.call-update) | async-done | bytes 2654224 | tf_op jit(solution)/shard_map/all_gather | solution.py:112
  130.1 0.0 copy-start
  130.1 2.0 copy-done
  132.1 1.4 shard_map.77
  133.5 0.0 copy-start.3
  133.5 18.0 %all_to_all.32 = bf16[4,144,288]{2,1,0:T(8,128)(2,1)S(1)} all-to-all(bf16[4,144,288]{2,1,0:T(8,128)(2,1)S(1)} %shard_map.77), channel_id=1, replica_groups=mesh['xh'=2,'z2'=2,'z1'=2,'z0'=2,'y2'=2,'y1'=2,'y0'=2,'core'=2,'rep'=2] ..., dimensions={0} | all-to-all | bytes 663552 | tf_op jit(solution)/shard_map/all_to_all | solution.py:92
  151.6 0.1 convert_reduce_fusion.1
  151.6 0.0 copy-done.4
  151.6 0.0 copy-done.5
  151.7 0.9 divide_convert_fusion
  152.5 0.1 broadcast_in_dim.5
  152.6 0.0 copy-start.1
  152.6 14.6 %all_to_all.33 = bf16[8,144,288]{2,1,0:T(8,128)(2,1)S(1)} all-to-all(bf16[8,144,288]{2,1,0:T(8,128)(2,1)S(1)} %broadcast_in_dim.5), channel_id=1, replica_groups=mesh['xh'=2,'z2'=2,'z1'=2,'z0'=2,'y2'=2,'y1'=2,'y0'=2,'core'=2,'rep'=2] ..., dimensions={0} | all-to-all | bytes 1327104 | tf_op jit(solution)/shard_map/all_to_all | solution.py:97
  167.2 0.0 copy-done.3
  167.2 1.4 shard_map.78
  168.6 13.3 %all_to_all.34 = bf16[4,144,288]{2,1,0:T(8,128)(2,1)} all-to-all(bf16[4,144,288]{2,1,0:T(8,128)(2,1)S(1)} %shard_map.78), channel_id=1, replica_groups=mesh['xh'=2,'z2'=2,'z1'=2,'z0'=2,'y2'=2,'y1'=2,'y0'=2,'core'=2,'rep'=2] ..., dimensions={0} | all-to-all | bytes 663552 | tf_op jit(solution)/shard_map/all_to_all | solution.py:92
  181.9 1.8 reduce_sum.44
  183.7 16.3 %all-gather.4 = bf16[576,288]{1,0:T(8,128)(2,1)S(1)} all-gather(bf16[144,288]{1,0:T(8,128)(2,1)} %reduce_sum.44), channel_id=6, replica_groups=mesh['xh'=2,'z2'=2,'z1'=2,'z0'=2,'y2'=2,'y1'=2,'y0'=2,'core'=2,'rep'=2] ..., dimensions={0}, use_global_device_ids=true | all-gather | bytes 414720 | tf_op jit(solution)/shard_map/all_gather | solution.py:136
  200.0 0.0 copy-done.1
  200.0 1.6 shard_map.79
  201.6 20.6 %all_to_all.35 = bf16[4,144,288]{2,1,0:T(8,128)(2,1)S(1)} all-to-all(bf16[4,144,288]{2,1,0:T(8,128)(2,1)S(1)} %shard_map.79), channel_id=1, replica_groups=mesh['xh'=2,'z2'=2,'z1'=2,'z0'=2,'y2'=2,'y1'=2,'y0'=2,'core'=2,'rep'=2] ..., dimensions={0} | all-to-all | bytes 663552 | tf_op jit(solution)/shard_map/all_to_all | solution.py:92
  222.2 0.7 convert_reduce_fusion
  (1 shorter events, 0.0 us)
Async XLA Ops:
  7.2 71.6 %all-gather.8.cloned.1.call-start = ((), (), s32[]{:S(2)}) async-start(), calls=%async_computation.6 | async-start | bytes 1880064 | tf_op jit(solution)/shard_map/all_gather | solution.py:107
  7.2 8.0 %collective-permute-start = (bf16[144,288]{1,0:T(8,128)(2,1)}, bf16[144,288]{1,0:T(8,128)(2,1)S(1)}, u32[]{:S(2)}, u32[]{:S(2)}) collective-permute-start(bf16[144,288]{1,0:T(8,128)(2,1)} %param.6), channel_id=1, source_target_pairs={{0,0},{1,1},{2,32},{3,33},{4,4},{5,5},{6,36},{7,37},{8,8},{9,9},{1... | collective-permute-start | bytes 248840 | tf_op jit(solution)/shard_map/ppermute | solution.py:31
  15.2 0.6 copy-start.6
  15.9 114.2 %all-gather.10.cloned.1.call-start = ((), (), s32[]{:S(2)}) async-start(), calls=%async_computation.7 | async-start | bytes 3981312 | tf_op jit(solution)/shard_map/all_gather | solution.py:112
  16.0 1.6 collective-permute-start.2
  48.8 5.5 %collective-permute-start.1 = (bf16[144,288]{1,0:T(8,128)(2,1)S(1)}, bf16[144,288]{1,0:T(8,128)(2,1)S(1)}, u32[]{:S(2)}, u32[]{:S(2)}) collective-permute-start(bf16[144,288]{1,0:T(8,128)(2,1)S(1)} %dynamic-slice_bitcast_fusion), channel_id=1, source_target_pairs={{0,1},{1,0},{2,3},{3,2},{4,5},{5,4},{6,7},{7,6},{8,9},{9,8},{10,11... | collective-permute-start | bytes 248840 | tf_op jit(solution)/shard_map/ppermute | solution.py:31
  78.8 1.5 copy-start.2
  106.5 45.2 %copy-start.4 = (f32[144,288]{1,0:T(8,128)S(1)}, f32[144,288]{1,0:T(8,128)}, u32[]{:S(2)}) copy-start(f32[144,288]{1,0:T(8,128)} %param.9) | copy-start | bytes 497668
  106.5 45.2 %copy-start.5 = (f32[144,288]{1,0:T(8,128)S(1)}, f32[144,288]{1,0:T(8,128)}, u32[]{:S(2)}) copy-start(f32[144,288]{1,0:T(8,128)} %param.8) | copy-start | bytes 497668
  130.1 2.0 copy-start
  133.5 33.7 %copy-start.3 = (bf16[2304,288]{1,0:T(8,128)(2,1)S(1)}, bf16[2304,288]{1,0:T(8,128)(2,1)}, u32[]{:S(2)}) copy-start(bf16[2304,288]{1,0:T(8,128)(2,1)} %all-gather.8.cloned.1.call-done) | copy-start | bytes 3981316
  152.6 47.4 %copy-start.1 = (bf16[32,144,288]{2,1,0:T(8,128)(2,1)S(1)}, bf16[32,144,288]{2,1,0:T(8,128)(2,1)}, u32[]{:S(2)}) copy-start(bf16[32,144,288]{2,1,0:T(8,128)(2,1)} %all-gather.10.cloned.1.call-done) | copy-start | bytes 7962628
Sparse Core Ops, SparseCore 0:
  16.0 54.2 all-gather.7
  72.4 57.6 all-gather.9

commit v3 on v2

--- a/solution.py
+++ b/solution.py
@@ -58,7 +58,7 @@
         total = None
         for k in range(4):
             part = jnp.dot(
-                rotated_ref[k], right_ref[block % 2, k, block // 2],
+                rotated_ref[k], right_ref[k % 2, block, k // 2],
                 preferred_element_type=F32,
             )
             total = part if total is None else total + part
@@ -81,7 +81,7 @@
         total = None
         for k in range(4):
             part = lax.dot_general(
-                back_ref[k], right_ref[k % 2, block, k // 2], (((1,), (1,)), ((), ())),
+                back_ref[k], right_ref[block % 2, k, block // 2], (((1,), (1,)), ((), ())),
                 preferred_element_type=F32,
             )
             total = part if total is None else total + part
@@ -107,23 +107,24 @@
     left = lax.all_gather(left, ("y2", "y1", "y0", "core"))
     left = left.reshape(2, 4, 2, half, width)
 
-    right = move(basis_right, [("xh", "y2"), ("z2", "y1")])
+    own = lax.dynamic_slice_in_dim(grad, rep * half, half, 0)
+    other = lax.dynamic_slice_in_dim(grad, (1 - rep) * half, half, 0)
+    other = move(other, [], ["rep"])
+    right = move(basis_right, [("z1", "y0"), ("z0", "core")])
+    other, right = lax.optimization_barrier((other, right))
     right = lax.all_gather(right, ("xh", "rep"))
     right = lax.all_gather(right, ("z2", "z1", "z0"))
     right = right.reshape(2, 4, 2, width, width)
-
-    own = lax.dynamic_slice_in_dim(grad, rep * half, half, 0)
-    other = lax.dynamic_slice_in_dim(grad, (1 - rep) * half, half, 0)
-    grad_half = (own.astype(F32) + move(other, [], ["rep"]).astype(F32)).astype(BF16)
+    grad_half = (own.astype(F32) + other.astype(F32)).astype(BF16)
 
     grad_panel = spread(grad_half, ("z2", "z1"))
     parts = call(first_kernel, (4, width, width), left, grad_panel)
     parts = parts.reshape(8, half, width)
     rotated = exchange(parts, ("xh", "z0", "rep")).astype(BF16)
 
-    rotated_panel = lax.all_gather(rotated, ("y0", "core"))
+    rotated_panel = lax.all_gather(rotated, ("y2", "y1"))
     parts = call(second_kernel, (4, half, width), rotated_panel, right)
-    projected = exchange(parts, ("y2", "y1"))
+    projected = exchange(parts, ("y0", "core"))
 
     new_first = BETA_ONE * first_moment + (1.0 - BETA_ONE) * projected
     new_second = BETA_TWO * second_moment + (1.0 - BETA_TWO) * projected * projected
@@ -133,9 +134,9 @@
     parts = call(third_kernel, (4, half, width), left, normed_panel)
     back_left = exchange(parts, ("z2", "z1")).astype(BF16)
 
-    back_panel = lax.all_gather(back_left, ("y2", "y1"))
+    back_panel = lax.all_gather(back_left, ("y0", "core"))
     parts = call(fourth_kernel, (4, half, width), back_panel, right)
-    update = exchange(parts, ("y0", "core"))
+    update = exchange(parts, ("y2", "y1"))
     return (update, new_first, new_second)
 
 

time: 230 us -> 216 us (0.939)
  blocking collectives: 180 us -> 142 us
  waiting for transfers between devices: 10.8 us -> 30.1 us
  starting transfers between devices: 9.3 us -> 12.5 us
    all_gather x1, waiting for transfers between devices: 4.94 us -> 24.2 us  [on_device(): right = lax.all_gather(right, ('z2', 'z1', 'z0'))]
    all_to_all x4, blocking collectives: 76.7 us -> 57.8 us  [exchange(): return jnp.sum(lax.all_to_all(parts, axes, 0, 0).astype(F32), axis=0)]
    all_gather x1, blocking collectives: 30.4 us -> 18.5 us  [on_device(): right = lax.all_gather(right, ('xh', 'rep'))]
    all_gather x2, blocking collectives: 34.9 us -> 24.7 us  [the longest x1 12.6 us: on_device(): back_panel = lax.all_gather(back_left, ('y0', 'core'))]
    ppermute x3, starting transfers between devices: 9.22 us -> 12.4 us  [move(): return lax.ppermute(block, BITS, pairs)]
    all_to_all x2, blocking collectives: 38.1 us -> 40.9 us  [spread(): lax.all_to_all(jnp.broadcast_to(block[None], (copies,) + block.shape), ax...]
  transfers between devices with their start and end apart: 5 -> 5, of which waited for: 3 -> 5; matrix products, arithmetic and copies ran while one was open for 1% -> 1% of each run, Pallas kernels for 1% -> 1%
where the time goes in v3:
time: 216 us; the launch traced here: 214 us
  blocking collectives  142 us (66%)
  waiting for transfers between devices  30.1 us (14%)
  between operations  14.2 us (7%)
  starting transfers between devices  12.5 us (6%)
  Pallas kernels  5.83 us (3%)
  local copies, waits for them, and re-layouts  5.17 us (2%)
  other arithmetic  4.53 us (2%)
    all_to_all x4, blocking collectives, exchange(): return jnp.sum(lax.all_to_all(parts, axes, 0, 0).astype(F32), axis=0)  57.8 us
    all_to_all x2, blocking collectives, spread(): lax.all_to_all(jnp.broadcast_to(block[None], (copies,) + block.shape), ax...  40.9 us
    all_gather x1, waiting for transfers between devices, on_device(): right = lax.all_gather(right, ('z2', 'z1', 'z0'))  24.2 us
    all_gather x1, blocking collectives, on_device(): right = lax.all_gather(right, ('xh', 'rep'))  18.5 us
    all_gather x1, blocking collectives, on_device(): back_panel = lax.all_gather(back_left, ('y0', 'core'))  12.6 us
    ppermute x3, starting transfers between devices, move(): return lax.ppermute(block, BITS, pairs)  12.4 us
    all_gather x1, blocking collectives, on_device(): rotated_panel = lax.all_gather(rotated, ('y2', 'y1'))  12.1 us
    pallas_call x4, Pallas kernels, call(): pl.pallas_call(kernel, out_shape=jax.ShapeDtypeStruct(out_shape, BF16), i...  5.83 us
  transfers between devices with their start and end apart: 5, of which 5 were waited for; matrix products, arithmetic and copies ran while one was open for 1% of the time, Pallas kernels for 1%

profile of v3, /device:TPU:1, one launch (start us, length us, event | category | flops | bytes accessed | tf_op | source)
XLA Modules:
  0.0 214.3 jit_solution(3338458044894316168)
XLA Ops:
  7.2 0.0 all-gather.8.cloned.1.call-start
  7.2 5.4 %collective-permute-start = (bf16[144,288]{1,0:T(8,128)(2,1)}, bf16[144,288]{1,0:T(8,128)(2,1)S(1)}, u32[]{:S(2)}, u32[]{:S(2)}) collective-permute-start(bf16[144,288]{1,0:T(8,128)(2,1)} %param.6), channel_id=1, source_target_pairs={{0,0},{1,1},{2,32},{3,33},{4,4},{5,5},{6,36},{7,37},{8,8},{9,9},{1... | collective-permute-start | bytes 248840 | tf_op jit(solution)/shard_map/ppermute | solution.py:31
  12.6 2.6 %collective-permute-done = bf16[144,288]{1,0:T(8,128)(2,1)S(1)} collective-permute-done((bf16[144,288]{1,0:T(8,128)(2,1)}, bf16[144,288]{1,0:T(8,128)(2,1)S(1)}, u32[]{:S(2)}, u32[]{:S(2)}) %collective-permute-start) | collective-permute-done | bytes 82976 | tf_op jit(solution)/shard_map/ppermute | solution.py:31
  15.2 0.0 copy-start.6
  15.2 0.6 copy-done.6
  15.9 0.0 all-gather.8.cloned.1.call-update
  15.9 0.0 all-gather.10.cloned.1.call-start
  16.0 0.9 dynamic-slice_bitcast_fusion
  16.9 3.1 %collective-permute-start.1 = (bf16[144,288]{1,0:T(8,128)(2,1)S(1)}, bf16[144,288]{1,0:T(8,128)(2,1)S(1)}, u32[]{:S(2)}, u32[]{:S(2)}) collective-permute-start(bf16[144,288]{1,0:T(8,128)(2,1)S(1)} %dynamic-slice_bitcast_fusion), channel_id=1, source_target_pairs={{0,1},{1,0},{2,3},{3,2},{4,5},{5,4},{6,7},{7,6},{8,9},{9,8},{10,11... | collective-permute-start | bytes 248840 | tf_op jit(solution)/shard_map/ppermute | solution.py:31
  20.0 3.9 %collective-permute-start.2 = (bf16[144,288]{1,0:T(8,128)(2,1)}, bf16[144,288]{1,0:T(8,128)(2,1)S(1)}, u32[]{:S(2)}, u32[]{:S(2)}) collective-permute-start(bf16[144,288]{1,0:T(8,128)(2,1)} %param.7), channel_id=1, source_target_pairs={{0,0},{1,1},{2,32},{3,33},{4,64},{5,65},{6,96},{7,97},{8,8},{9,9},... | collective-permute-start | bytes 248840 | tf_op jit(solution)/shard_map/ppermute | solution.py:31
  23.9 1.1 collective-permute-done.1
  25.0 1.5 collective-permute-done.2
  26.6 18.5 %all-gather.2 = bf16[576,288]{1,0:T(8,128)(2,1)} all-gather(bf16[144,288]{1,0:T(8,128)(2,1)S(1)} %collective-permute-done.2), channel_id=4, replica_groups=mesh['xh'=2,'z2'=2,'z1'=2,'z0'=2,'y2'=2,'y1'=2,'y0'=2,'core'=2,'rep'=2] ..., dimensions={0}, use_global_device_ids=true | all-gather | bytes 414720 | tf_op jit(solution)/shard_map/all_gather | solution.py:115
  45.1 0.0 all-gather.10.cloned.1.call-update
  45.1 0.9 fusion.1
  46.1 23.4 %all_to_all.30.grad_ref = bf16[4,144,288]{2,1,0:T(8,128)(2,1)S(1)} all-to-all(bf16[4,144,288]{2,1,0:T(8,128)(2,1)S(1)} %broadcast_in_dim.4), channel_id=1, replica_groups=mesh['xh'=2,'z2'=2,'z1'=2,'z0'=2,'y2'=2,'y1'=2,'y0'=2,'core'=2,'rep'=2] ..., dimensions={0} | all-to-all | bytes 663552 | tf_op jit(solution)/shard_map/all_to_all | solution.py:97
  69.6 0.6 all-gather.8.cloned.1.call-done
  70.1 0.0 copy-start.2
  70.1 1.5 copy-done.2
  71.6 1.4 shard_map.76
  73.1 14.5 %all_to_all.31 = bf16[8,144,288]{2,1,0:T(8,128)(2,1)S(1)} all-to-all(bf16[8,144,288]{2,1,0:T(8,128)(2,1)S(1)} %bitcast.17), channel_id=1, replica_groups=mesh['xh'=2,'z2'=2,'z1'=2,'z0'=2,'y2'=2,'y1'=2,'y0'=2,'core'=2,'rep'=2] ..., dimensions={0} | all-to-all | bytes 1327104 | tf_op jit(solution)/shard_map/all_to_all | solution.py:92
  87.6 0.0 copy-start.4
  87.6 0.0 copy-start.5
  87.6 0.1 reduce_sum.42
  87.8 12.1 %all-gather.1 = bf16[576,288]{1,0:T(8,128)(2,1)S(1)} all-gather(bf16[144,288]{1,0:T(8,128)(2,1)S(1)} %reduce_sum.42), channel_id=3, replica_groups=mesh['xh'=2,'z2'=2,'z1'=2,'z0'=2,'y2'=2,'y1'=2,'y0'=2,'core'=2,'rep'=2] ..., dimensions={0}, use_global_device_ids=true | all-gather | bytes 414720 | tf_op jit(solution)/shard_map/all_gather | solution.py:125
  99.9 24.2 %all-gather.10.cloned.1.call-done = bf16[32,144,288]{2,1,0:T(8,128)(2,1)} async-done(((bf16[4,144,288]{2,1,0:T(8,128)(2,1)}), bf16[32,144,288]{2,1,0:T(8,128)(2,1)}) %all-gather.10.cloned.1.call-update) | async-done | bytes 2654224 | tf_op jit(solution)/shard_map/all_gather | solution.py:116
  124.1 0.0 copy-start
  124.1 2.0 copy-done
  126.1 1.4 shard_map.77
  127.4 0.0 copy-start.3
  127.5 10.8 %all_to_all.32 = bf16[4,144,288]{2,1,0:T(8,128)(2,1)S(1)} all-to-all(bf16[4,144,288]{2,1,0:T(8,128)(2,1)S(1)} %shard_map.77), channel_id=1, replica_groups=mesh['xh'=2,'z2'=2,'z1'=2,'z0'=2,'y2'=2,'y1'=2,'y0'=2,'core'=2,'rep'=2] ..., dimensions={0} | all-to-all | bytes 663552 | tf_op jit(solution)/shard_map/all_to_all | solution.py:92
  138.2 0.1 convert_reduce_fusion.1
  138.3 0.0 copy-done.4
  138.3 0.0 copy-done.5
  138.3 0.9 divide_convert_fusion
  139.2 0.1 broadcast_in_dim.5
  139.3 0.0 copy-start.1
  139.3 17.5 %all_to_all.33 = bf16[8,144,288]{2,1,0:T(8,128)(2,1)S(1)} all-to-all(bf16[8,144,288]{2,1,0:T(8,128)(2,1)S(1)} %broadcast_in_dim.5), channel_id=1, replica_groups=mesh['xh'=2,'z2'=2,'z1'=2,'z0'=2,'y2'=2,'y1'=2,'y0'=2,'core'=2,'rep'=2] ..., dimensions={0} | all-to-all | bytes 1327104 | tf_op jit(solution)/shard_map/all_to_all | solution.py:97
  156.8 0.0 copy-done.3
  156.8 1.4 shard_map.78
  158.2 15.5 %all_to_all.34 = bf16[4,144,288]{2,1,0:T(8,128)(2,1)} all-to-all(bf16[4,144,288]{2,1,0:T(8,128)(2,1)S(1)} %shard_map.78), channel_id=1, replica_groups=mesh['xh'=2,'z2'=2,'z1'=2,'z0'=2,'y2'=2,'y1'=2,'y0'=2,'core'=2,'rep'=2] ..., dimensions={0} | all-to-all | bytes 663552 | tf_op jit(solution)/shard_map/all_to_all | solution.py:92
  173.6 1.8 reduce_sum.44
  175.4 12.6 %all-gather.4 = bf16[576,288]{1,0:T(8,128)(2,1)S(1)} all-gather(bf16[144,288]{1,0:T(8,128)(2,1)} %reduce_sum.44), channel_id=6, replica_groups=mesh['xh'=2,'z2'=2,'z1'=2,'z0'=2,'y2'=2,'y1'=2,'y0'=2,'core'=2,'rep'=2] ..., dimensions={0}, use_global_device_ids=true | all-gather | bytes 414720 | tf_op jit(solution)/shard_map/all_gather | solution.py:137
  188.0 0.0 copy-done.1
  188.0 1.6 shard_map.79
  189.6 17.1 %all_to_all.35 = bf16[4,144,288]{2,1,0:T(8,128)(2,1)S(1)} all-to-all(bf16[4,144,288]{2,1,0:T(8,128)(2,1)S(1)} %shard_map.79), channel_id=1, replica_groups=mesh['xh'=2,'z2'=2,'z1'=2,'z0'=2,'y2'=2,'y1'=2,'y0'=2,'core'=2,'rep'=2] ..., dimensions={0} | all-to-all | bytes 663552 | tf_op jit(solution)/shard_map/all_to_all | solution.py:92
  206.7 0.7 convert_reduce_fusion
  (1 shorter events, 0.0 us)
Async XLA Ops:
  7.2 63.0 %all-gather.8.cloned.1.call-start = ((), (), s32[]{:S(2)}) async-start(), calls=%async_computation.6 | async-start | bytes 1880064 | tf_op jit(solution)/shard_map/all_gather | solution.py:107
  7.2 8.0 %collective-permute-start = (bf16[144,288]{1,0:T(8,128)(2,1)}, bf16[144,288]{1,0:T(8,128)(2,1)S(1)}, u32[]{:S(2)}, u32[]{:S(2)}) collective-permute-start(bf16[144,288]{1,0:T(8,128)(2,1)} %param.6), channel_id=1, source_target_pairs={{0,0},{1,1},{2,32},{3,33},{4,4},{5,5},{6,36},{7,37},{8,8},{9,9},{1... | collective-permute-start | bytes 248840 | tf_op jit(solution)/shard_map/ppermute | solution.py:31
  15.2 0.6 copy-start.6
  15.9 108.2 %all-gather.10.cloned.1.call-start = ((), (), s32[]{:S(2)}) async-start(), calls=%async_computation.7 | async-start | bytes 3981312 | tf_op jit(solution)/shard_map/all_gather | solution.py:116
  16.9 8.2 %collective-permute-start.1 = (bf16[144,288]{1,0:T(8,128)(2,1)S(1)}, bf16[144,288]{1,0:T(8,128)(2,1)S(1)}, u32[]{:S(2)}, u32[]{:S(2)}) collective-permute-start(bf16[144,288]{1,0:T(8,128)(2,1)S(1)} %dynamic-slice_bitcast_fusion), channel_id=1, source_target_pairs={{0,1},{1,0},{2,3},{3,2},{4,5},{5,4},{6,7},{7,6},{8,9},{9,8},{10,11... | collective-permute-start | bytes 248840 | tf_op jit(solution)/shard_map/ppermute | solution.py:31
  20.0 6.6 %collective-permute-start.2 = (bf16[144,288]{1,0:T(8,128)(2,1)}, bf16[144,288]{1,0:T(8,128)(2,1)S(1)}, u32[]{:S(2)}, u32[]{:S(2)}) collective-permute-start(bf16[144,288]{1,0:T(8,128)(2,1)} %param.7), channel_id=1, source_target_pairs={{0,0},{1,1},{2,32},{3,33},{4,64},{5,65},{6,96},{7,97},{8,8},{9,9},... | collective-permute-start | bytes 248840 | tf_op jit(solution)/shard_map/ppermute | solution.py:31
  70.1 1.5 copy-start.2
  87.6 50.7 %copy-start.4 = (f32[144,288]{1,0:T(8,128)S(1)}, f32[144,288]{1,0:T(8,128)}, u32[]{:S(2)}) copy-start(f32[144,288]{1,0:T(8,128)} %param.9) | copy-start | bytes 497668
  87.6 50.7 %copy-start.5 = (f32[144,288]{1,0:T(8,128)S(1)}, f32[144,288]{1,0:T(8,128)}, u32[]{:S(2)}) copy-start(f32[144,288]{1,0:T(8,128)} %param.8) | copy-start | bytes 497668
  124.1 2.0 copy-start
  127.4 29.3 %copy-start.3 = (bf16[2304,288]{1,0:T(8,128)(2,1)S(1)}, bf16[2304,288]{1,0:T(8,128)(2,1)}, u32[]{:S(2)}) copy-start(bf16[2304,288]{1,0:T(8,128)(2,1)} %all-gather.8.cloned.1.call-done) | copy-start | bytes 3981316
  139.3 48.7 %copy-start.1 = (bf16[32,144,288]{2,1,0:T(8,128)(2,1)S(1)}, bf16[32,144,288]{2,1,0:T(8,128)(2,1)}, u32[]{:S(2)}) copy-start(bf16[32,144,288]{2,1,0:T(8,128)(2,1)} %all-gather.10.cloned.1.call-done) | copy-start | bytes 7962628
Sparse Core Ops, SparseCore 0:
  16.0 54.0 all-gather.7
  72.2 51.8 all-gather.9

commit v4 on v3

--- a/solution.py
+++ b/solution.py
@@ -54,11 +54,11 @@
 
 
 def second_kernel(rotated_ref, right_ref, out_ref):
-    for block in range(4):
+    for block in range(2):
         total = None
-        for k in range(4):
+        for k in range(8):
             part = jnp.dot(
-                rotated_ref[k], right_ref[k % 2, block, k // 2],
+                rotated_ref[k], right_ref[k % 4, block, k // 4],
                 preferred_element_type=F32,
             )
             total = part if total is None else total + part
@@ -66,22 +66,23 @@
 
 
 def third_kernel(left_ref, normed_ref, out_ref):
-    for block in range(4):
-        total = None
-        for k in range(4):
-            part = jnp.dot(
-                left_ref[k // 2, block, k % 2], normed_ref[k], preferred_element_type=F32
-            )
-            total = part if total is None else total + part
-        out_ref[block] = total.astype(BF16)
+    rows, width = left_ref.shape[3:]
+    total = None
+    for k in range(4):
+        part = jnp.dot(
+            left_ref[k // 2, :, k % 2].reshape(4 * rows, width), normed_ref[k],
+            preferred_element_type=F32,
+        )
+        total = part if total is None else total + part
+    out_ref[...] = total.astype(BF16).reshape(4, rows, width)
 
 
 def fourth_kernel(back_ref, right_ref, out_ref):
-    for block in range(4):
+    for block in range(8):
         total = None
-        for k in range(4):
+        for k in range(2):
             part = lax.dot_general(
-                back_ref[k], right_ref[block % 2, k, block // 2], (((1,), (1,)), ((), ())),
+                back_ref[k], right_ref[block % 4, k, block // 4], (((1,), (1,)), ((), ())),
                 preferred_element_type=F32,
             )
             total = part if total is None else total + part
@@ -110,11 +111,11 @@
     own = lax.dynamic_slice_in_dim(grad, rep * half, half, 0)
     other = lax.dynamic_slice_in_dim(grad, (1 - rep) * half, half, 0)
     other = move(other, [], ["rep"])
-    right = move(basis_right, [("z1", "y0"), ("z0", "core")])
+    right = move(basis_right, [("z0", "core")])
     other, right = lax.optimization_barrier((other, right))
     right = lax.all_gather(right, ("xh", "rep"))
     right = lax.all_gather(right, ("z2", "z1", "z0"))
-    right = right.reshape(2, 4, 2, width, width)
+    right = right.reshape(4, 2, 2, width, width)
     grad_half = (own.astype(F32) + other.astype(F32)).astype(BF16)
 
     grad_panel = spread(grad_half, ("z2", "z1"))
@@ -122,9 +123,9 @@
     parts = parts.reshape(8, half, width)
     rotated = exchange(parts, ("xh", "z0", "rep")).astype(BF16)
 
-    rotated_panel = lax.all_gather(rotated, ("y2", "y1"))
-    parts = call(second_kernel, (4, half, width), rotated_panel, right)
-    projected = exchange(parts, ("y0", "core"))
+    rotated_panel = lax.all_gather(rotated, ("y2", "y1", "y0"))
+    parts = call(second_kernel, (2, half, width), rotated_panel, right)
+    projected = exchange(parts, ("core",))
 
     new_first = BETA_ONE * first_moment + (1.0 - BETA_ONE) * projected
     new_second = BETA_TWO * second_moment + (1.0 - BETA_TWO) * projected * projected
@@ -134,9 +135,9 @@
     parts = call(third_kernel, (4, half, width), left, normed_panel)
     back_left = exchange(parts, ("z2", "z1")).astype(BF16)
 
-    back_panel = lax.all_gather(back_left, ("y0", "core"))
-    parts = call(fourth_kernel, (4, half, width), back_panel, right)
-    update = exchange(parts, ("y2", "y1"))
+    back_panel = lax.all_gather(back_left, ("core",))
+    parts = call(fourth_kernel, (8, half, width), back_panel, right)
+    update = exchange(parts, ("y2", "y1", "y0"))
     return (update, new_first, new_second)
 
 

time: 216 us -> 215 us (level)
  blocking collectives: 142 us -> 157 us
  waiting for transfers between devices: 30.1 us -> 15.6 us
    all_gather x1, waiting for transfers between devices: 24.2 us -> 8.02 us  [on_device(): right = lax.all_gather(right, ('z2', 'z1', 'z0'))]
    all_to_all x4, blocking collectives: 57.8 us -> 68.7 us  [exchange(): return jnp.sum(lax.all_to_all(parts, axes, 0, 0).astype(F32), axis=0)]
    all_gather x2, blocking collectives: 24.7 us -> 30.2 us  [the longest x1 22.3 us: on_device(): rotated_panel = lax.all_gather(rotated, ('y2', 'y1', 'y0'))]
where the time goes in v4:
time: 215 us; the launch traced here: 214 us
  blocking collectives  157 us (73%)
  waiting for transfers between devices  15.6 us (7%)
  between operations  14.2 us (7%)
  starting transfers between devices  12.5 us (6%)
  Pallas kernels  5.7 us (3%)
  local copies, waits for them, and re-layouts  5.17 us (2%)
  other arithmetic  4.56 us (2%)
    all_to_all x4, blocking collectives, exchange(): return jnp.sum(lax.all_to_all(parts, axes, 0, 0).astype(F32), axis=0)  68.7 us
    all_to_all x2, blocking collectives, spread(): lax.all_to_all(jnp.broadcast_to(block[None], (copies,) + block.shape), ax...  39.1 us
    all_gather x1, blocking collectives, on_device(): rotated_panel = lax.all_gather(rotated, ('y2', 'y1', 'y0'))  22.3 us
    all_gather x1, blocking collectives, on_device(): right = lax.all_gather(right, ('xh', 'rep'))  18.5 us
    ppermute x3, starting transfers between devices, move(): return lax.ppermute(block, BITS, pairs)  12.4 us
    all_gather x1, waiting for transfers between devices, on_device(): right = lax.all_gather(right, ('z2', 'z1', 'z0'))  8.02 us
    all_gather x1, blocking collectives, on_device(): back_panel = lax.all_gather(back_left, ('core',))  7.88 us
    pallas_call x4, Pallas kernels, call(): pl.pallas_call(kernel, out_shape=jax.ShapeDtypeStruct(out_shape, BF16), i...  5.7 us
  transfers between devices with their start and end apart: 5, of which 5 were waited for; matrix products, arithmetic and copies ran while one was open for 1% of the time, Pallas kernels for 1%

profile of v4, /device:TPU:1, one launch (start us, length us, event | category | flops | bytes accessed | tf_op | source)
XLA Modules:
  0.0 214.3 jit_solution(1867795224148735456)
XLA Ops:
  7.2 0.0 all-gather.8.cloned.1.call-start
  7.2 5.4 %collective-permute-start = (bf16[144,288]{1,0:T(8,128)(2,1)}, bf16[144,288]{1,0:T(8,128)(2,1)S(1)}, u32[]{:S(2)}, u32[]{:S(2)}) collective-permute-start(bf16[144,288]{1,0:T(8,128)(2,1)} %param.6), channel_id=1, source_target_pairs={{0,0},{1,1},{2,32},{3,33},{4,4},{5,5},{6,36},{7,37},{8,8},{9,9},{1... | collective-permute-start | bytes 248840 | tf_op jit(solution)/shard_map/ppermute | solution.py:31
  12.6 2.6 %collective-permute-done = bf16[144,288]{1,0:T(8,128)(2,1)S(1)} collective-permute-done((bf16[144,288]{1,0:T(8,128)(2,1)}, bf16[144,288]{1,0:T(8,128)(2,1)S(1)}, u32[]{:S(2)}, u32[]{:S(2)}) %collective-permute-start) | collective-permute-done | bytes 82976 | tf_op jit(solution)/shard_map/ppermute | solution.py:31
  15.2 0.0 copy-start.6
  15.2 0.6 copy-done.6
  15.9 0.0 all-gather.8.cloned.1.call-update
  15.9 0.0 all-gather.10.cloned.1.call-start
  16.0 0.9 dynamic-slice_bitcast_fusion
  16.9 3.1 %collective-permute-start.1 = (bf16[144,288]{1,0:T(8,128)(2,1)S(1)}, bf16[144,288]{1,0:T(8,128)(2,1)S(1)}, u32[]{:S(2)}, u32[]{:S(2)}) collective-permute-start(bf16[144,288]{1,0:T(8,128)(2,1)S(1)} %dynamic-slice_bitcast_fusion), channel_id=1, source_target_pairs={{0,1},{1,0},{2,3},{3,2},{4,5},{5,4},{6,7},{7,6},{8,9},{9,8},{10,11... | collective-permute-start | bytes 248840 | tf_op jit(solution)/shard_map/ppermute | solution.py:31
  20.0 3.9 %collective-permute-start.2 = (bf16[144,288]{1,0:T(8,128)(2,1)}, bf16[144,288]{1,0:T(8,128)(2,1)S(1)}, u32[]{:S(2)}, u32[]{:S(2)}) collective-permute-start(bf16[144,288]{1,0:T(8,128)(2,1)} %param.7), channel_id=1, source_target_pairs={{0,0},{1,1},{2,32},{3,33},{4,4},{5,5},{6,36},{7,37},{8,8},{9,9},{1... | collective-permute-start | bytes 248840 | tf_op jit(solution)/shard_map/ppermute | solution.py:31
  23.9 1.1 collective-permute-done.1
  25.0 1.5 collective-permute-done.2
  26.6 18.5 %all-gather.2 = bf16[576,288]{1,0:T(8,128)(2,1)} all-gather(bf16[144,288]{1,0:T(8,128)(2,1)S(1)} %collective-permute-done.2), channel_id=4, replica_groups=mesh['xh'=2,'z2'=2,'z1'=2,'z0'=2,'y2'=2,'y1'=2,'y0'=2,'core'=2,'rep'=2] ..., dimensions={0}, use_global_device_ids=true | all-gather | bytes 414720 | tf_op jit(solution)/shard_map/all_gather | solution.py:116
  45.1 0.0 all-gather.10.cloned.1.call-update
  45.1 0.9 fusion.1
  46.1 21.6 %all_to_all.30.grad_ref = bf16[4,144,288]{2,1,0:T(8,128)(2,1)S(1)} all-to-all(bf16[4,144,288]{2,1,0:T(8,128)(2,1)S(1)} %broadcast_in_dim.4), channel_id=1, replica_groups=mesh['xh'=2,'z2'=2,'z1'=2,'z0'=2,'y2'=2,'y1'=2,'y0'=2,'core'=2,'rep'=2] ..., dimensions={0} | all-to-all | bytes 663552 | tf_op jit(solution)/shard_map/all_to_all | solution.py:98
  67.7 2.3 %all-gather.8.cloned.1.call-done = bf16[2304,288]{1,0:T(8,128)(2,1)} async-done(((bf16[144,288]{1,0:T(8,128)(2,1)}), bf16[2304,288]{1,0:T(8,128)(2,1)}) %all-gather.8.cloned.1.call-update) | async-done | bytes 1327120 | tf_op jit(solution)/shard_map/all_gather | solution.py:108
  70.1 0.0 copy-start.2
  70.1 1.5 copy-done.2
  71.5 1.4 shard_map.76
  73.0 20.5 %all_to_all.31 = bf16[8,144,288]{2,1,0:T(8,128)(2,1)S(1)} all-to-all(bf16[8,144,288]{2,1,0:T(8,128)(2,1)S(1)} %bitcast.17), channel_id=1, replica_groups=mesh['xh'=2,'z2'=2,'z1'=2,'z0'=2,'y2'=2,'y1'=2,'y0'=2,'core'=2,'rep'=2] ..., dimensions={0} | all-to-all | bytes 1327104 | tf_op jit(solution)/shard_map/all_to_all | solution.py:93
  93.5 0.1 reduce_sum.42
  93.7 22.3 %all-gather.1 = bf16[1152,288]{1,0:T(8,128)(2,1)S(1)} all-gather(bf16[144,288]{1,0:T(8,128)(2,1)S(1)} %reduce_sum.42), channel_id=3, replica_groups=mesh['xh'=2,'z2'=2,'z1'=2,'z0'=2,'y2'=2,'y1'=2,'y0'=2,'core'=2,'rep'=2] ..., dimensions={0}, use_global_device_ids=true | all-gather | bytes 746496 | tf_op jit(solution)/shard_map/all_gather | solution.py:126
  116.0 8.0 %all-gather.10.cloned.1.call-done = bf16[32,144,288]{2,1,0:T(8,128)(2,1)} async-done(((bf16[4,144,288]{2,1,0:T(8,128)(2,1)}), bf16[32,144,288]{2,1,0:T(8,128)(2,1)}) %all-gather.10.cloned.1.call-update) | async-done | bytes 2654224 | tf_op jit(solution)/shard_map/all_gather | solution.py:117
  124.0 0.0 copy-start
  124.0 2.0 copy-done
  126.0 0.0 copy-start.4
  126.0 0.0 copy-start.5
  126.0 1.4 shard_map.77
  127.4 4.4 %all_to_all.32 = bf16[2,144,288]{2,1,0:T(8,128)(2,1)S(1)} all-to-all(bf16[2,144,288]{2,1,0:T(8,128)(2,1)S(1)} %shard_map.77), channel_id=1, replica_groups=mesh['xh'=2,'z2'=2,'z1'=2,'z0'=2,'y2'=2,'y1'=2,'y0'=2,'core'=2,'rep'=2] ..., dimensions={0} | all-to-all | bytes 331776 | tf_op jit(solution)/shard_map/all_to_all | solution.py:93
  131.8 0.0 copy-done.4
  131.8 0.0 copy-done.5
  131.8 0.0 copy-start.3
  131.8 0.9 divide_convert_fusion
  132.7 0.1 broadcast_in_dim.5
  132.8 17.5 %all_to_all.33 = bf16[8,144,288]{2,1,0:T(8,128)(2,1)S(1)} all-to-all(bf16[8,144,288]{2,1,0:T(8,128)(2,1)S(1)} %broadcast_in_dim.5), channel_id=1, replica_groups=mesh['xh'=2,'z2'=2,'z1'=2,'z0'=2,'y2'=2,'y1'=2,'y0'=2,'core'=2,'rep'=2] ..., dimensions={0} | all-to-all | bytes 1327104 | tf_op jit(solution)/shard_map/all_to_all | solution.py:98
  150.2 0.0 copy-done.3
  150.2 0.0 copy-start.1
  150.3 1.2 shard_map.78
  151.5 15.7 %all_to_all.34 = bf16[4,144,288]{2,1,0:T(8,128)(2,1)} all-to-all(bf16[4,144,288]{2,1,0:T(8,128)(2,1)S(1)} %shard_map.78), channel_id=1, replica_groups=mesh['xh'=2,'z2'=2,'z1'=2,'z0'=2,'y2'=2,'y1'=2,'y0'=2,'core'=2,'rep'=2] ..., dimensions={0} | all-to-all | bytes 663552 | tf_op jit(solution)/shard_map/all_to_all | solution.py:93
  167.2 1.8 reduce_sum.44
  168.9 7.9 %all-gather.4 = bf16[288,288]{1,0:T(8,128)(2,1)S(1)} all-gather(bf16[144,288]{1,0:T(8,128)(2,1)} %reduce_sum.44), channel_id=6, replica_groups=mesh['xh'=2,'z2'=2,'z1'=2,'z0'=2,'y2'=2,'y1'=2,'y0'=2,'core'=2,'rep'=2] ..., dimensions={0}, use_global_device_ids=true | all-gather | bytes 248832 | tf_op jit(solution)/shard_map/all_gather | solution.py:138
  176.8 0.0 copy-done.1
  176.8 1.6 shard_map.79
  178.4 28.2 %all_to_all.35 = bf16[8,144,288]{2,1,0:T(8,128)(2,1)S(1)} all-to-all(bf16[8,144,288]{2,1,0:T(8,128)(2,1)S(1)} %shard_map.79), channel_id=1, replica_groups=mesh['xh'=2,'z2'=2,'z1'=2,'z0'=2,'y2'=2,'y1'=2,'y0'=2,'core'=2,'rep'=2] ..., dimensions={0} | all-to-all | bytes 1327104 | tf_op jit(solution)/shard_map/all_to_all | solution.py:93
  206.6 0.8 convert_reduce_fusion
  (2 shorter events, 0.1 us)
Async XLA Ops:
  7.2 62.9 %all-gather.8.cloned.1.call-start = ((), (), s32[]{:S(2)}) async-start(), calls=%async_computation.6 | async-start | bytes 1880064 | tf_op jit(solution)/shard_map/all_gather | solution.py:108
  7.2 8.0 %collective-permute-start = (bf16[144,288]{1,0:T(8,128)(2,1)}, bf16[144,288]{1,0:T(8,128)(2,1)S(1)}, u32[]{:S(2)}, u32[]{:S(2)}) collective-permute-start(bf16[144,288]{1,0:T(8,128)(2,1)} %param.6), channel_id=1, source_target_pairs={{0,0},{1,1},{2,32},{3,33},{4,4},{5,5},{6,36},{7,37},{8,8},{9,9},{1... | collective-permute-start | bytes 248840 | tf_op jit(solution)/shard_map/ppermute | solution.py:31
  15.2 0.6 copy-start.6
  15.9 108.1 %all-gather.10.cloned.1.call-start = ((), (), s32[]{:S(2)}) async-start(), calls=%async_computation.7 | async-start | bytes 3981312 | tf_op jit(solution)/shard_map/all_gather | solution.py:117
  16.9 8.2 %collective-permute-start.1 = (bf16[144,288]{1,0:T(8,128)(2,1)S(1)}, bf16[144,288]{1,0:T(8,128)(2,1)S(1)}, u32[]{:S(2)}, u32[]{:S(2)}) collective-permute-start(bf16[144,288]{1,0:T(8,128)(2,1)S(1)} %dynamic-slice_bitcast_fusion), channel_id=1, source_target_pairs={{0,1},{1,0},{2,3},{3,2},{4,5},{5,4},{6,7},{7,6},{8,9},{9,8},{10,11... | collective-permute-start | bytes 248840 | tf_op jit(solution)/shard_map/ppermute | solution.py:31
  20.0 6.6 %collective-permute-start.2 = (bf16[144,288]{1,0:T(8,128)(2,1)}, bf16[144,288]{1,0:T(8,128)(2,1)S(1)}, u32[]{:S(2)}, u32[]{:S(2)}) collective-permute-start(bf16[144,288]{1,0:T(8,128)(2,1)} %param.7), channel_id=1, source_target_pairs={{0,0},{1,1},{2,32},{3,33},{4,4},{5,5},{6,36},{7,37},{8,8},{9,9},{1... | collective-permute-start | bytes 248840 | tf_op jit(solution)/shard_map/ppermute | solution.py:31
  70.1 1.5 copy-start.2
  124.0 2.0 copy-start
  126.0 5.8 %copy-start.4 = (f32[144,288]{1,0:T(8,128)S(1)}, f32[144,288]{1,0:T(8,128)}, u32[]{:S(2)}) copy-start(f32[144,288]{1,0:T(8,128)} %param.9) | copy-start | bytes 497668
  126.0 5.8 %copy-start.5 = (f32[144,288]{1,0:T(8,128)S(1)}, f32[144,288]{1,0:T(8,128)}, u32[]{:S(2)}) copy-start(f32[144,288]{1,0:T(8,128)} %param.8) | copy-start | bytes 497668
  131.8 18.4 %copy-start.3 = (bf16[2304,288]{1,0:T(8,128)(2,1)S(1)}, bf16[2304,288]{1,0:T(8,128)(2,1)}, u32[]{:S(2)}) copy-start(bf16[2304,288]{1,0:T(8,128)(2,1)} %all-gather.8.cloned.1.call-done) | copy-start | bytes 3981316
  150.2 26.6 %copy-start.1 = (bf16[32,144,288]{2,1,0:T(8,128)(2,1)S(1)}, bf16[32,144,288]{2,1,0:T(8,128)(2,1)}, u32[]{:S(2)}) copy-start(bf16[32,144,288]{2,1,0:T(8,128)(2,1)} %all-gather.10.cloned.1.call-done) | copy-start | bytes 7962628
Sparse Core Ops, SparseCore 0:
  16.0 53.9 all-gather.7
  72.1 51.8 all-gather.9

commit v5 on v4

--- a/solution.py
+++ b/solution.py
@@ -53,16 +53,40 @@
         out_ref[block] = total.astype(BF16)
 
 
-def second_kernel(rotated_ref, right_ref, out_ref):
+def second_kernel(rotated_ref, right_ref, out_ref, held_ref, sems):
+    copies = [
+        pltpu.make_async_copy(right_ref.at[:, block], held_ref.at[block], sems.at[block])
+        for block in range(2)
+    ]
+    for copy in copies:
+        copy.start()
     for block in range(2):
+        copies[block].wait()
         total = None
         for k in range(8):
             part = jnp.dot(
-                rotated_ref[k], right_ref[k % 4, block, k // 4],
-                preferred_element_type=F32,
+                rotated_ref[k], held_ref[block, k % 4, k // 4], preferred_element_type=F32
             )
             total = part if total is None else total + part
         out_ref[block] = total.astype(BF16)
+
+
+def second(rotated, right):
+    _, rows, width = rotated.shape
+    return pl.pallas_call(
+        second_kernel,
+        out_shape=jax.ShapeDtypeStruct((2, rows, width), BF16),
+        in_specs=[
+            pl.BlockSpec(memory_space=pltpu.VMEM),
+            pl.BlockSpec(memory_space=pltpu.HBM),
+        ],
+        out_specs=pl.BlockSpec(memory_space=pltpu.VMEM),
+        scratch_shapes=[
+            pltpu.VMEM((2, 4, 2, width, width), BF16),
+            pltpu.SemaphoreType.DMA((2,)),
+        ],
+        compiler_params=pltpu.CompilerParams(vmem_limit_bytes=32 * 2**20),
+    )(rotated, right)
 
 
 def third_kernel(left_ref, normed_ref, out_ref):
@@ -124,8 +148,9 @@
     rotated = exchange(parts, ("xh", "z0", "rep")).astype(BF16)
 
     rotated_panel = lax.all_gather(rotated, ("y2", "y1", "y0"))
-    parts = call(second_kernel, (2, half, width), rotated_panel, right)
+    parts = second(rotated_panel, right)
     projected = exchange(parts, ("core",))
+    right, projected = lax.optimization_barrier((right, projected))
 
     new_first = BETA_ONE * first_moment + (1.0 - BETA_ONE) * projected
     new_second = BETA_TWO * second_moment + (1.0 - BETA_TWO) * projected * projected

time: 215 us -> 215 us (level)
    pallas_call x4 -> x3, Pallas kernels: 5.7 us -> 4.29 us  [call(): pl.pallas_call(kernel, out_shape=jax.ShapeDtypeStruct(out_shape, BF16), i...]
where the time goes in v5:
time: 215 us
  blocking collectives  157 us (73%)
  waiting for transfers between devices  15.6 us (7%)
  between operations  14.2 us (7%)
  starting transfers between devices  12.5 us (6%)
  Pallas kernels  6.22 us (3%)
  local copies, waits for them, and re-layouts  5.17 us (2%)
  other arithmetic  4.56 us (2%)
    all_to_all x4, blocking collectives, exchange(): return jnp.sum(lax.all_to_all(parts, axes, 0, 0).astype(F32), axis=0)  68.7 us
    all_to_all x2, blocking collectives, spread(): lax.all_to_all(jnp.broadcast_to(block[None], (copies,) + block.shape), ax...  39.1 us
    all_gather x1, blocking collectives, on_device(): rotated_panel = lax.all_gather(rotated, ('y2', 'y1', 'y0'))  22.3 us
    all_gather x1, blocking collectives, on_device(): right = lax.all_gather(right, ('xh', 'rep'))  18.5 us
    ppermute x3, starting transfers between devices, move(): return lax.ppermute(block, BITS, pairs)  12.4 us
    all_gather x1, waiting for transfers between devices, on_device(): right = lax.all_gather(right, ('z2', 'z1', 'z0'))  8.02 us
    all_gather x1, blocking collectives, on_device(): back_panel = lax.all_gather(back_left, ('core',))  7.88 us
    ppermute x3, waiting for transfers between devices, move(): return lax.ppermute(block, BITS, pairs)  5.26 us
  transfers between devices with their start and end apart: 5, of which 5 were waited for; matrix products, arithmetic and copies ran while one was open for 1% of the time, Pallas kernels for 1%

profile of v5, /device:TPU:1, one launch (start us, length us, event | category | flops | bytes accessed | tf_op | source)
XLA Modules:
  0.0 214.8 jit_solution(17120498387879869472)
XLA Ops:
  7.2 0.0 all-gather.8.cloned.1.call-start
  7.2 5.4 %collective-permute-start = (bf16[144,288]{1,0:T(8,128)(2,1)}, bf16[144,288]{1,0:T(8,128)(2,1)S(1)}, u32[]{:S(2)}, u32[]{:S(2)}) collective-permute-start(bf16[144,288]{1,0:T(8,128)(2,1)} %param.6), channel_id=1, source_target_pairs={{0,0},{1,1},{2,32},{3,33},{4,4},{5,5},{6,36},{7,37},{8,8},{9,9},{1... | collective-permute-start | bytes 248840 | tf_op jit(solution)/shard_map/ppermute | solution.py:31
  12.6 2.6 %collective-permute-done = bf16[144,288]{1,0:T(8,128)(2,1)S(1)} collective-permute-done((bf16[144,288]{1,0:T(8,128)(2,1)}, bf16[144,288]{1,0:T(8,128)(2,1)S(1)}, u32[]{:S(2)}, u32[]{:S(2)}) %collective-permute-start) | collective-permute-done | bytes 82976 | tf_op jit(solution)/shard_map/ppermute | solution.py:31
  15.2 0.0 copy-start.6
  15.2 0.6 copy-done.6
  15.9 0.0 all-gather.8.cloned.1.call-update
  15.9 0.0 all-gather.10.cloned.1.call-start
  16.0 0.9 dynamic-slice_bitcast_fusion
  16.9 3.1 %collective-permute-start.1 = (bf16[144,288]{1,0:T(8,128)(2,1)S(1)}, bf16[144,288]{1,0:T(8,128)(2,1)S(1)}, u32[]{:S(2)}, u32[]{:S(2)}) collective-permute-start(bf16[144,288]{1,0:T(8,128)(2,1)S(1)} %dynamic-slice_bitcast_fusion), channel_id=1, source_target_pairs={{0,1},{1,0},{2,3},{3,2},{4,5},{5,4},{6,7},{7,6},{8,9},{9,8},{10,11... | collective-permute-start | bytes 248840 | tf_op jit(solution)/shard_map/ppermute | solution.py:31
  20.0 3.9 %collective-permute-start.2 = (bf16[144,288]{1,0:T(8,128)(2,1)}, bf16[144,288]{1,0:T(8,128)(2,1)S(1)}, u32[]{:S(2)}, u32[]{:S(2)}) collective-permute-start(bf16[144,288]{1,0:T(8,128)(2,1)} %param.7), channel_id=1, source_target_pairs={{0,0},{1,1},{2,32},{3,33},{4,4},{5,5},{6,36},{7,37},{8,8},{9,9},{1... | collective-permute-start | bytes 248840 | tf_op jit(solution)/shard_map/ppermute | solution.py:31
  23.9 1.1 collective-permute-done.1
  25.0 1.5 collective-permute-done.2
  26.6 18.5 %all-gather.1 = bf16[576,288]{1,0:T(8,128)(2,1)} all-gather(bf16[144,288]{1,0:T(8,128)(2,1)S(1)} %collective-permute-done.2), channel_id=3, replica_groups=mesh['xh'=2,'z2'=2,'z1'=2,'z0'=2,'y2'=2,'y1'=2,'y0'=2,'core'=2,'rep'=2] ..., dimensions={0}, use_global_device_ids=true | all-gather | bytes 414720 | tf_op jit(solution)/shard_map/all_gather | solution.py:140
  45.1 0.0 all-gather.10.cloned.1.call-update
  45.1 0.9 fusion.1
  46.1 21.6 %all_to_all.30.grad_ref = bf16[4,144,288]{2,1,0:T(8,128)(2,1)S(1)} all-to-all(bf16[4,144,288]{2,1,0:T(8,128)(2,1)S(1)} %broadcast_in_dim.4), channel_id=1, replica_groups=mesh['xh'=2,'z2'=2,'z1'=2,'z0'=2,'y2'=2,'y1'=2,'y0'=2,'core'=2,'rep'=2] ..., dimensions={0} | all-to-all | bytes 663552 | tf_op jit(solution)/shard_map/all_to_all | solution.py:122
  67.7 2.3 %all-gather.8.cloned.1.call-done = bf16[2304,288]{1,0:T(8,128)(2,1)} async-done(((bf16[144,288]{1,0:T(8,128)(2,1)}), bf16[2304,288]{1,0:T(8,128)(2,1)}) %all-gather.8.cloned.1.call-update) | async-done | bytes 1327120 | tf_op jit(solution)/shard_map/all_gather | solution.py:132
  70.1 0.0 copy-start.2
  70.1 1.5 copy-done.2
  71.5 1.4 shard_map.76
  73.0 20.5 %all_to_all.31 = bf16[8,144,288]{2,1,0:T(8,128)(2,1)S(1)} all-to-all(bf16[8,144,288]{2,1,0:T(8,128)(2,1)S(1)} %bitcast.17), channel_id=1, replica_groups=mesh['xh'=2,'z2'=2,'z1'=2,'z0'=2,'y2'=2,'y1'=2,'y0'=2,'core'=2,'rep'=2] ..., dimensions={0} | all-to-all | bytes 1327104 | tf_op jit(solution)/shard_map/all_to_all | solution.py:117
  93.5 0.1 reduce_sum.42
  93.7 22.3 %all-gather.3 = bf16[1152,288]{1,0:T(8,128)(2,1)S(1)} all-gather(bf16[144,288]{1,0:T(8,128)(2,1)S(1)} %reduce_sum.42), channel_id=5, replica_groups=mesh['xh'=2,'z2'=2,'z1'=2,'z0'=2,'y2'=2,'y1'=2,'y0'=2,'core'=2,'rep'=2] ..., dimensions={0}, use_global_device_ids=true | all-gather | bytes 746496 | tf_op jit(solution)/shard_map/all_gather | solution.py:150
  116.0 8.0 %all-gather.10.cloned.1.call-done = bf16[32,144,288]{2,1,0:T(8,128)(2,1)} async-done(((bf16[4,144,288]{2,1,0:T(8,128)(2,1)}), bf16[32,144,288]{2,1,0:T(8,128)(2,1)}) %all-gather.10.cloned.1.call-update) | async-done | bytes 2654224 | tf_op jit(solution)/shard_map/all_gather | solution.py:141
  124.0 0.0 copy-start
  124.0 2.0 copy-done
  126.0 0.0 copy-start.4
  126.0 0.0 copy-start.5
  126.0 1.9 shard_map.77
  127.9 4.4 %all_to_all.32 = bf16[2,144,288]{2,1,0:T(8,128)(2,1)S(1)} all-to-all(bf16[2,144,288]{2,1,0:T(8,128)(2,1)S(1)} %shard_map.77), channel_id=1, replica_groups=mesh['xh'=2,'z2'=2,'z1'=2,'z0'=2,'y2'=2,'y1'=2,'y0'=2,'core'=2,'rep'=2] ..., dimensions={0} | all-to-all | bytes 331776 | tf_op jit(solution)/shard_map/all_to_all | solution.py:117
  132.3 0.0 copy-done.4
  132.3 0.0 copy-done.5
  132.3 0.0 copy-start.3
  132.3 0.9 divide_convert_fusion
  133.2 0.1 broadcast_in_dim.5
  133.3 17.5 %all_to_all.33 = bf16[8,144,288]{2,1,0:T(8,128)(2,1)S(1)} all-to-all(bf16[8,144,288]{2,1,0:T(8,128)(2,1)S(1)} %broadcast_in_dim.5), channel_id=1, replica_groups=mesh['xh'=2,'z2'=2,'z1'=2,'z0'=2,'y2'=2,'y1'=2,'y0'=2,'core'=2,'rep'=2] ..., dimensions={0} | all-to-all | bytes 1327104 | tf_op jit(solution)/shard_map/all_to_all | solution.py:122
  150.8 0.0 copy-done.3
  150.8 0.0 copy-start.1
  150.8 1.2 shard_map.78
  152.0 15.7 %all_to_all.34 = bf16[4,144,288]{2,1,0:T(8,128)(2,1)} all-to-all(bf16[4,144,288]{2,1,0:T(8,128)(2,1)S(1)} %shard_map.78), channel_id=1, replica_groups=mesh['xh'=2,'z2'=2,'z1'=2,'z0'=2,'y2'=2,'y1'=2,'y0'=2,'core'=2,'rep'=2] ..., dimensions={0} | all-to-all | bytes 663552 | tf_op jit(solution)/shard_map/all_to_all | solution.py:117
  167.7 1.8 reduce_sum.44
  169.4 7.9 %all-gather.4 = bf16[288,288]{1,0:T(8,128)(2,1)S(1)} all-gather(bf16[144,288]{1,0:T(8,128)(2,1)} %reduce_sum.44), channel_id=6, replica_groups=mesh['xh'=2,'z2'=2,'z1'=2,'z0'=2,'y2'=2,'y1'=2,'y0'=2,'core'=2,'rep'=2] ..., dimensions={0}, use_global_device_ids=true | all-gather | bytes 248832 | tf_op jit(solution)/shard_map/all_gather | solution.py:163
  177.3 0.0 copy-done.1
  177.3 1.6 shard_map.79
  179.0 28.1 %all_to_all.35 = bf16[8,144,288]{2,1,0:T(8,128)(2,1)S(1)} all-to-all(bf16[8,144,288]{2,1,0:T(8,128)(2,1)S(1)} %shard_map.79), channel_id=1, replica_groups=mesh['xh'=2,'z2'=2,'z1'=2,'z0'=2,'y2'=2,'y1'=2,'y0'=2,'core'=2,'rep'=2] ..., dimensions={0} | all-to-all | bytes 1327104 | tf_op jit(solution)/shard_map/all_to_all | solution.py:117
  207.1 0.8 convert_reduce_fusion
  (2 shorter events, 0.1 us)
Async XLA Ops:
  7.2 62.9 %all-gather.8.cloned.1.call-start = ((), (), s32[]{:S(2)}) async-start(), calls=%async_computation.6 | async-start | bytes 1880064 | tf_op jit(solution)/shard_map/all_gather | solution.py:132
  7.2 8.0 %collective-permute-start = (bf16[144,288]{1,0:T(8,128)(2,1)}, bf16[144,288]{1,0:T(8,128)(2,1)S(1)}, u32[]{:S(2)}, u32[]{:S(2)}) collective-permute-start(bf16[144,288]{1,0:T(8,128)(2,1)} %param.6), channel_id=1, source_target_pairs={{0,0},{1,1},{2,32},{3,33},{4,4},{5,5},{6,36},{7,37},{8,8},{9,9},{1... | collective-permute-start | bytes 248840 | tf_op jit(solution)/shard_map/ppermute | solution.py:31
  15.2 0.6 copy-start.6
  15.9 108.1 %all-gather.10.cloned.1.call-start = ((), (), s32[]{:S(2)}) async-start(), calls=%async_computation.7 | async-start | bytes 3981312 | tf_op jit(solution)/shard_map/all_gather | solution.py:141
  16.9 8.2 %collective-permute-start.1 = (bf16[144,288]{1,0:T(8,128)(2,1)S(1)}, bf16[144,288]{1,0:T(8,128)(2,1)S(1)}, u32[]{:S(2)}, u32[]{:S(2)}) collective-permute-start(bf16[144,288]{1,0:T(8,128)(2,1)S(1)} %dynamic-slice_bitcast_fusion), channel_id=1, source_target_pairs={{0,1},{1,0},{2,3},{3,2},{4,5},{5,4},{6,7},{7,6},{8,9},{9,8},{10,11... | collective-permute-start | bytes 248840 | tf_op jit(solution)/shard_map/ppermute | solution.py:31
  20.0 6.6 %collective-permute-start.2 = (bf16[144,288]{1,0:T(8,128)(2,1)}, bf16[144,288]{1,0:T(8,128)(2,1)S(1)}, u32[]{:S(2)}, u32[]{:S(2)}) collective-permute-start(bf16[144,288]{1,0:T(8,128)(2,1)} %param.7), channel_id=1, source_target_pairs={{0,0},{1,1},{2,32},{3,33},{4,4},{5,5},{6,36},{7,37},{8,8},{9,9},{1... | collective-permute-start | bytes 248840 | tf_op jit(solution)/shard_map/ppermute | solution.py:31
  70.1 1.5 copy-start.2
  124.0 2.0 copy-start
  126.0 6.3 %copy-start.4 = (f32[144,288]{1,0:T(8,128)S(1)}, f32[144,288]{1,0:T(8,128)}, u32[]{:S(2)}) copy-start(f32[144,288]{1,0:T(8,128)} %param.9) | copy-start | bytes 497668
  126.0 6.3 %copy-start.5 = (f32[144,288]{1,0:T(8,128)S(1)}, f32[144,288]{1,0:T(8,128)}, u32[]{:S(2)}) copy-start(f32[144,288]{1,0:T(8,128)} %param.8) | copy-start | bytes 497668
  132.3 18.4 %copy-start.3 = (bf16[2304,288]{1,0:T(8,128)(2,1)S(1)}, bf16[2304,288]{1,0:T(8,128)(2,1)}, u32[]{:S(2)}) copy-start(bf16[2304,288]{1,0:T(8,128)(2,1)} %all-gather.8.cloned.1.call-done) | copy-start | bytes 3981316
  150.8 26.6 %copy-start.1 = (bf16[32,144,288]{2,1,0:T(8,128)(2,1)S(1)}, bf16[32,144,288]{2,1,0:T(8,128)(2,1)}, u32[]{:S(2)}) copy-start(bf16[32,144,288]{2,1,0:T(8,128)(2,1)} %all-gather.10.cloned.1.call-done) | copy-start | bytes 7962628
Sparse Core Ops, SparseCore 0:
  16.0 53.9 all-gather.7
  72.1 51.8 all-gather.9
